TPU v7x, 256 devices: a whole 4x4x8 slice. The times are simulated.
256 devices in a mesh: prompt: 16 (over x, z_hi), seq: 16 (over z_lo, y, core).
Axes of the slice: x: 4, y: 4, z: 8 (z_hi: 4, z_lo: 2; z = z_hi * 2 + z_lo), core: 2. Of those that a mesh axis runs over, the one named last changes fastest.
Arguments:
- queries: bfloat16 [16, 8192, 1024], P('prompt', 'seq'), may hold values from -5 to 5
- resp_kv: bfloat16 [16, 8192, 256], P('prompt', 'seq'), may hold values from -16 to 16
- prefix_kv: bfloat16 [16, 768, 256], P('prompt', 'seq'), may hold values from -16 to 16
- lengths: int32 [16, 16], P('prompt'), may hold values from 256 to 512, as said below
- upstream: bfloat16 [16, 8192, 1024], P('prompt', 'seq'), may hold values from -6 to 6
Outputs:
- attended: bfloat16 [16, 8192, 1024], P('prompt', 'seq')
- grad_queries: bfloat16 [16, 8192, 1024], P('prompt', 'seq')
- grad_resp_kv: float32 [16, 8192, 256], P('prompt', 'seq')
- grad_prefix_kv: float32 [16, 768, 256], P('prompt', 'seq')
Inputs may be any that keep to these rules, and one draw needn't show every extreme that they name: `lengths`: each prompt's 16 responses fill its slots in order from slot 0; one response of every prompt has exactly 512 tokens.
All inputs are finite; a program needn't handle non-finite values.
Results may differ from a plain program's by a relative error of at most 0.011.
Values may be sent and summed in bfloat16 or wider, within the bound.
No kernel may reach another device: no remote copies, remote signals or barrier semaphores. Data moves between devices by JAX's collectives and lax.ppermute only.
A program may use at most 192 MiB of HBM per device.

v0:
```python
import math

import jax
import jax.numpy as jnp
from jax import lax
from jax.sharding import PartitionSpec as P


def shifted(block, axis, distance):
    devices = range(lax.axis_size(axis))
    route = [(i - distance, i) for i in devices if i - distance in devices]
    return lax.ppermute(block, axis, route)


def slot_segments(resp_ends, slot_ids):
    counted = jnp.sum((slot_ids[:, None] >= resp_ends[None, :]).astype(jnp.int32), axis=1)
    return jnp.where(slot_ids < 0, -1, counted)


def block_terms(query_block, grad_block, key_part, value_part, visible, live_rows, score_scale):
    scores = (
        jnp.einsum("rgd,kd->rgk", query_block, key_part, preferred_element_type=jnp.float32)
        * score_scale
    )
    scores = jnp.where(visible[:, None, :], scores, -jnp.inf)
    row_max = jnp.max(scores, axis=-1, keepdims=True)
    weights = jnp.exp(scores - row_max)
    row_total = jnp.sum(weights, axis=-1, keepdims=True)
    mixed = (
        jnp.einsum(
            "rgk,kd->rgd",
            weights.astype(jnp.bfloat16),
            value_part,
            preferred_element_type=jnp.float32,
        )
        / row_total
    )
    attended = (mixed * live_rows[:, None, None]).astype(jnp.bfloat16)
    log_total = row_max + jnp.log(row_total)
    probs = jnp.exp(scores - log_total)
    delta = jnp.sum(
        grad_block.astype(jnp.float32) * attended.astype(jnp.float32), axis=-1, keepdims=True
    )
    dprobs = jnp.einsum("rgd,kd->rgk", grad_block, value_part, preferred_element_type=jnp.float32)
    dscores = (probs * (dprobs - delta)).astype(jnp.bfloat16)
    grad_query = (
        jnp.einsum("rgk,kd->rgd", dscores, key_part, preferred_element_type=jnp.float32)
        * score_scale
    ).astype(jnp.bfloat16)
    return (attended, grad_query, dscores, probs.astype(jnp.bfloat16))


def body(queries, resp_kv, prefix_kv, lengths, upstream):
    shard_rows = queries.shape[1]
    head_dim = resp_kv.shape[2] // 2
    head_count = queries.shape[2] // head_dim
    responses = lengths.shape[1]
    score_scale = head_dim ** (-0.5)
    shard_index = lax.axis_index("seq")
    resp_ends = jnp.cumsum(lengths[0])
    positions = shard_index * shard_rows + jnp.arange(shard_rows, dtype=jnp.int32)
    own_seg = slot_segments(resp_ends, positions)
    prev_seg = slot_segments(resp_ends, positions - shard_rows)
    live_rows = (own_seg < responses).astype(jnp.float32)
    live_total = lax.psum(jnp.sum(lengths[0]).astype(jnp.float32), "prompt")
    factor = jnp.float32(lax.axis_size("prompt") * lax.axis_size("seq") * shard_rows) / live_total
    prefix_all = lax.all_gather(prefix_kv[0], "seq", axis=0, tiled=True)
    previous = shifted(resp_kv[0], "seq", 1)
    prefix_len = prefix_all.shape[0]
    key_vals = jnp.concatenate([prefix_all, previous, resp_kv[0]], axis=0)
    key_slots = jnp.concatenate([positions - shard_rows, positions])
    key_segs = jnp.concatenate([prev_seg, own_seg])
    same_resp = (key_segs[None, :] == own_seg[:, None]) & (key_slots[None, :] <= positions[:, None])
    visible = jnp.concatenate([jnp.ones((shard_rows, prefix_len), jnp.bool_), same_resp], axis=1)
    key_part = key_vals[:, :head_dim]
    value_part = key_vals[:, head_dim:]
    query_three = queries[0].reshape(shard_rows, head_count, head_dim)
    scaled_live = factor * live_rows
    grad_out = (
        upstream[0].reshape(shard_rows, head_count, head_dim).astype(jnp.float32)
        * scaled_live[:, None, None]
    ).astype(jnp.bfloat16)
    head_group = math.gcd(head_count, max(1, 512 // shard_rows))
    out_parts = []
    query_grads = []
    key_grads = jnp.zeros((prefix_len + 2 * shard_rows, head_dim), jnp.float32)
    value_grads = jnp.zeros((prefix_len + 2 * shard_rows, head_dim), jnp.float32)
    for first_head in range(0, head_count, head_group):
        query_block = query_three[:, first_head : first_head + head_group]
        grad_block = grad_out[:, first_head : first_head + head_group]
        attended, grad_query, dscores, probs_low = block_terms(
            query_block, grad_block, key_part, value_part, visible, live_rows, score_scale
        )
        key_grads = key_grads + jnp.einsum(
            "rgk,rgd->kd", dscores, query_block, preferred_element_type=jnp.float32
        )
        value_grads = value_grads + jnp.einsum(
            "rgk,rgd->kd", probs_low, grad_block, preferred_element_type=jnp.float32
        )
        out_parts.append(attended)
        query_grads.append(grad_query)
    kv_grads = jnp.concatenate([key_grads * score_scale, value_grads], axis=1)
    prefix_grads = lax.psum_scatter(kv_grads[:prefix_len], "seq", scatter_dimension=0, tiled=True)
    prev_grads = kv_grads[prefix_len : prefix_len + shard_rows]
    own_grads = kv_grads[prefix_len + shard_rows :]
    returned = shifted(prev_grads.astype(jnp.bfloat16), "seq", -1).astype(prev_grads.dtype)
    grad_resp = own_grads + returned
    attended_all = jnp.concatenate(out_parts, axis=1).reshape(shard_rows, head_count * head_dim)
    query_grad_all = jnp.concatenate(query_grads, axis=1).reshape(shard_rows, head_count * head_dim)
    return (attended_all[None], query_grad_all[None], grad_resp[None], prefix_grads[None])


def solution(mesh):
    in_specs = (
        P("prompt", "seq", None),
        P("prompt", "seq", None),
        P("prompt", "seq", None),
        P("prompt", None),
        P("prompt", "seq", None),
    )
    out_specs = (
        P("prompt", "seq", None),
        P("prompt", "seq", None),
        P("prompt", "seq", None),
        P("prompt", "seq", None),
    )
    return jax.shard_map(body, mesh=mesh, in_specs=in_specs, out_specs=out_specs, check_vma=False)
```

profile of v0, /device:TPU:1, one launch (start us, length us, event | category | flops | bytes accessed | tf_op | source)
XLA Modules:
  0.0 201.4 jit_solution(9735265526432654468)
XLA Ops:
  7.2 4.6 %collective-permute-start = (bf16[512,256]{1,0:T(8,128)(2,1)}, bf16[512,256]{1,0:T(8,128)(2,1)S(1)}, u32[]{:S(2)}, u32[]{:S(2)}) collective-permute-start(bf16[512,256]{1,0:T(8,128)(2,1)} %bitcast.216), channel_id=1, source_target_pairs={{0,1},{1,2},{2,3},{3,4},{4,5},{5,6},{6,7},{7,8},{8,9},{9,10},{10,1... | collective-permute-start | bytes 786440 | tf_op jit(solution)/shard_map/ppermute | solution.py:12
  11.8 1.3 reduce_sum.181
  13.8 41.1 %psum.7 = f32[]{:T(128)} all-reduce(f32[]{:T(128)S(6)} %convert_element_type.306), channel_id=1, replica_groups=mesh['prompt'=16,'seq'=16] {'prompt'}, use_global_device_ids=true, to_apply=%region_20.21 | all-reduce | flops 1 | bytes 8 | tf_op jit(solution)/shard_map/psum | solution.py:65
  54.9 0.7 copy.83
  55.9 26.3 %all-gather = bf16[1,768,256]{2,1,0:T(8,128)(2,1)S(1)} all-gather(bf16[1,48,256]{2,1,0:T(8,128)(2,1)} %param.7), channel_id=2, replica_groups=mesh['prompt'=16,'seq'=16] {'seq'}, dimensions={1}, use_global_device_ids=true | all-gather | bytes 417792 | tf_op jit(solution)/shard_map/all_gather | solution.py:67
  82.2 2.6 %copy.93 = f32[1,512,1024]{1,2,0:T(8,128)} copy(bf16[1,512,1024]{2,1,0:T(8,128)(2,1)} %param.9) | data formatting | bytes 3145728 | tf_op jit(solution)/shard_map/convert_element_type | solution.py:80
  85.5 1.9 multiply_convert_fusion.8
  87.4 1.5 copy.84
  88.9 0.8 compare_and_fusion
  90.5 1.1 pad_maximum_fusion
  104.0 0.9 constant_dynamic-update-slice_fusion.4
  107.7 0.8 fusion.32
  108.8 0.8 multiply_convert_fusion.7
  110.3 1.1 fusion.161
  111.4 0.8 convolution_add_fusion.6
  112.2 0.8 convolution_add_fusion.5
  113.0 0.8 convolution_add_fusion.4
  113.8 0.8 convolution_add_fusion.3
  114.5 0.8 convolution_add_fusion.2
  115.3 0.8 convolution_add_fusion.1
  116.1 0.8 multiply_convert_fusion.1
  116.9 0.8 multiply_convert_fusion.2
  117.7 0.8 multiply_convert_fusion.3
  118.6 0.8 multiply_convert_fusion.4
  119.4 1.0 multiply_convert_fusion.5
  120.4 0.8 multiply_convert_fusion.6
  121.3 0.8 convolution_add_fusion
  122.0 0.8 multiply_convert_fusion
  123.3 0.7 convolution_add_fusion.13
  124.7 0.7 convolution_add_fusion.11
  125.5 0.7 convolution_add_fusion.10
  127.0 0.7 convolution_add_fusion.8
  127.7 0.7 fusion.24
  128.5 0.9 pad_maximum_fusion.1
  129.4 2.3 %copy.102 = bf16[1,512,1024]{2,1,0:T(8,128)(2,1)} copy(bf16[1,512,1024]{1,2,0:T(8,128)(2,1)} %bitcast.214) | data formatting | bytes 2097152
  131.7 2.7 %fusion.159 = bf16[512,8,128]{0,2,1:T(8,128)(2,1)} fusion(bf16[512,8,128]{0,2,1:T(8,128)(2,1)} %fusion.161, bf16[512,1792]{0,1:T(8,128)(2,1)} %copy-done.11, bf16[1792,256]{1,0:T(8,128)(2,1)S(1)} %pad_maximum_fusion), kind=kOutput, calls=%fused_computation.155 | convolution fusion | flops 235012096 | bytes 2424832 | tf_op jit(solution)/shard_map/rgk,kd->rgd/dot_general | solution.py:47
  134.4 1.1 fusion.157
  135.6 2.1 %collective-permute-start.1 = (bf16[512,256]{0,1:T(8,128)(2,1)S(1)}, bf16[512,256]{0,1:T(8,128)(2,1)S(1)}, u32[]{:S(2)}, u32[]{:S(2)}) collective-permute-start(bf16[512,256]{0,1:T(8,128)(2,1)S(1)} %fusion.187), channel_id=1, source_target_pairs={{1,0},{2,1},{3,2},{4,3},{5,4},{6,5},{7,6},{8,7},{9,8},{10,9},{11,1... | collective-permute-start | bytes 786440 | tf_op jit(solution)/shard_map/ppermute | solution.py:12
  137.6 2.3 %copy.114 = f32[768,256]{1,0:T(8,128)} copy(f32[768,256]{0,1:T(8,128)} %pad_maximum_fusion.1) | data formatting | bytes 1572864
  140.0 2.8 %fusion.155 = bf16[512,8,128]{0,2,1:T(8,128)(2,1)} fusion(bf16[512,8,128]{0,2,1:T(8,128)(2,1)} %fusion.157, bf16[512,1792]{0,1:T(8,128)(2,1)} %copy-done.6, bf16[1792,256]{1,0:T(8,128)(2,1)S(1)} %pad_maximum_fusion), kind=kOutput, calls=%fused_computation.151 | convolution fusion | flops 235012096 | bytes 2424832 | tf_op jit(solution)/shard_map/rgk,kd->rgd/dot_general | solution.py:47
  142.7 1.1 fusion.153
  143.9 1.1 fusion.151
  145.0 1.1 fusion.149
  146.1 1.1 fusion.147
  147.2 2.3 %copy.103 = bf16[1,512,1024]{2,1,0:T(8,128)(2,1)} copy(bf16[1,512,1024]{1,2,0:T(8,128)(2,1)} %bitcast.213) | data formatting | bytes 2097152
  149.6 1.0 copy.104
  150.6 42.4 %reduce-scatter.4.cloned.1.call-done = f32[48,256]{1,0:T(8,128)} async-done(((f32[768,256]{1,0:T(8,128)}), f32[48,256]{1,0:T(8,128)}) %reduce-scatter.4.cloned.1.call-update) | async-done | bytes 49168
  192.9 0.9 copy.115
  (83 shorter events, 19.9 us)
Async XLA Ops:
  7.2 185.8 %reduce-scatter.4.cloned.1.call-start = ((), (), s32[]{:S(2)}) async-start(), calls=%async_computation.1 | async-start | bytes 835584
  7.2 82.6 %collective-permute-start = (bf16[512,256]{1,0:T(8,128)(2,1)}, bf16[512,256]{1,0:T(8,128)(2,1)S(1)}, u32[]{:S(2)}, u32[]{:S(2)}) collective-permute-start(bf16[512,256]{1,0:T(8,128)(2,1)} %bitcast.216), channel_id=1, source_target_pairs={{0,1},{1,2},{2,3},{3,4},{4,5},{5,6},{6,7},{7,8},{8,9},{9,10},{10,1... | collective-permute-start | bytes 786440 | tf_op jit(solution)/shard_map/ppermute | solution.py:12
  88.9 20.7 %copy-start.12 = (bf16[1,512,1024]{1,2,0:T(8,128)(2,1)}, bf16[1,512,1024]{1,2,0:T(8,128)(2,1)S(1)}, u32[]{:S(2)}) copy-start(bf16[1,512,1024]{1,2,0:T(8,128)(2,1)S(1)} %copy.84) | copy-start | bytes 3145732
  89.8 0.7 copy-start.15
  107.7 1.9 copy-start.14
  116.9 10.1 %copy-start = (bf16[512,1792]{0,1:T(8,128)(2,1)}, bf16[512,1792]{0,1:T(8,128)(2,1)S(1)}, u32[]{:S(2)}) copy-start(bf16[512,1792]{0,1:T(8,128)(2,1)S(1)} %multiply_convert_fusion.1) | copy-start | bytes 5505028
  117.7 8.5 %copy-start.2 = (bf16[512,1792]{0,1:T(8,128)(2,1)}, bf16[512,1792]{0,1:T(8,128)(2,1)S(1)}, u32[]{:S(2)}) copy-start(bf16[512,1792]{0,1:T(8,128)(2,1)S(1)} %multiply_convert_fusion.2) | copy-start | bytes 5505028
  118.6 6.9 %copy-start.4 = (bf16[512,1792]{0,1:T(8,128)(2,1)}, bf16[512,1792]{0,1:T(8,128)(2,1)S(1)}, u32[]{:S(2)}) copy-start(bf16[512,1792]{0,1:T(8,128)(2,1)S(1)} %multiply_convert_fusion.3) | copy-start | bytes 5505028
  119.4 5.4 %copy-start.6 = (bf16[512,1792]{0,1:T(8,128)(2,1)}, bf16[512,1792]{0,1:T(8,128)(2,1)S(1)}, u32[]{:S(2)}) copy-start(bf16[512,1792]{0,1:T(8,128)(2,1)S(1)} %multiply_convert_fusion.4) | copy-start | bytes 5505028
  120.4 3.6 %copy-start.9 = (bf16[512,1792]{0,1:T(8,128)(2,1)}, bf16[512,1792]{0,1:T(8,128)(2,1)S(1)}, u32[]{:S(2)}) copy-start(bf16[512,1792]{0,1:T(8,128)(2,1)S(1)} %multiply_convert_fusion.5) | copy-start | bytes 5505028
  121.3 1.6 copy-start.11
  122.0 1.2 copy-start.13
  123.3 4.5 %copy-start.7 = (bf16[512,1792]{0,1:T(8,128)(2,1)}, bf16[512,1792]{0,1:T(8,128)(2,1)S(1)}, u32[]{:S(2)}) copy-start(bf16[512,1792]{0,1:T(8,128)(2,1)S(1)} %multiply_convert_fusion) | copy-start | bytes 5505028
  131.7 2.7 %copy-start.10 = (bf16[512,1792]{0,1:T(8,128)(2,1)S(1)}, bf16[512,1792]{0,1:T(8,128)(2,1)}, u32[]{:S(2)}) copy-start(bf16[512,1792]{0,1:T(8,128)(2,1)} %copy-done.9) | copy-start | bytes 5505028
  135.6 13.9 %collective-permute-start.1 = (bf16[512,256]{0,1:T(8,128)(2,1)S(1)}, bf16[512,256]{0,1:T(8,128)(2,1)S(1)}, u32[]{:S(2)}, u32[]{:S(2)}) collective-permute-start(bf16[512,256]{0,1:T(8,128)(2,1)S(1)} %fusion.187), channel_id=1, source_target_pairs={{1,0},{2,1},{3,2},{4,3},{5,4},{6,5},{7,6},{8,7},{9,8},{10,9},{11,1... | collective-permute-start | bytes 786440 | tf_op jit(solution)/shard_map/ppermute | solution.py:12
  140.0 2.8 %copy-start.5 = (bf16[512,1792]{0,1:T(8,128)(2,1)S(1)}, bf16[512,1792]{0,1:T(8,128)(2,1)}, u32[]{:S(2)}) copy-start(bf16[512,1792]{0,1:T(8,128)(2,1)} %copy-done.4) | copy-start | bytes 5505028
  140.0 3.9 %copy-start.3 = (bf16[512,1792]{0,1:T(8,128)(2,1)S(1)}, bf16[512,1792]{0,1:T(8,128)(2,1)}, u32[]{:S(2)}) copy-start(bf16[512,1792]{0,1:T(8,128)(2,1)} %copy-done.2) | copy-start | bytes 5505028
  142.7 2.2 %copy-start.1 = (bf16[512,1792]{0,1:T(8,128)(2,1)S(1)}, bf16[512,1792]{0,1:T(8,128)(2,1)}, u32[]{:S(2)}) copy-start(bf16[512,1792]{0,1:T(8,128)(2,1)} %copy-done) | copy-start | bytes 5505028
  143.9 2.2 %copy-start.8 = (bf16[512,1792]{0,1:T(8,128)(2,1)S(1)}, bf16[512,1792]{0,1:T(8,128)(2,1)}, u32[]{:S(2)}) copy-start(bf16[512,1792]{0,1:T(8,128)(2,1)} %copy-done.7) | copy-start | bytes 5505028
Sparse Core Ops, SparseCore 0:
  140.1 52.8 reduce-scatter.3
where the time goes:
time: 204 us; the launch traced here: 201 us
  blocking collectives  67.4 us (33%)
  waiting for transfers between devices  42.4 us (21%)
  matrix products  42.2 us (21%)
  between operations  15.9 us (8%)
  local copies, waits for them, and re-layouts  15.4 us (8%)
  other arithmetic  11.3 us (6%)
  starting transfers between devices  6.71 us (3%)
    unnamed x2, waiting for transfers between devices  42.4 us
    psum x1, blocking collectives, body(): live_total = lax.psum(jnp.sum(lengths[0]).astype(jnp.float32), 'prompt')  41.1 us
    all_gather x1, blocking collectives, body(): prefix_all = lax.all_gather(prefix_kv[0], 'seq', axis=0, tiled=True)  26.3 us
    dot_general x8, matrix products, block_terms(): jnp.einsum('rgk,kd->rgd', dscores, key_part, preferred_element_type=jnp.f...  12.2 us
    unnamed x39, local copies, waits for them, and re-layouts  12.1 us
    dot_general x8, matrix products, block_terms(): jnp.einsum('rgd,kd->rgk', grad_block, value_part, preferred_element_type=...  6.69 us
    ppermute x2, starting transfers between devices, shifted(): return lax.ppermute(block, axis, route)  6.67 us
    dot_general x8, matrix products, body(): jnp.einsum('rgk,rgd->kd', probs_low, grad_block, preferred_element_type=j...  6.13 us
  transfers between devices with their start and end apart: 3, of which 1 were waited for; matrix products, arithmetic and copies ran while one was open for 11% of the time, Pallas kernels for 0%

commit v1 on v0

v1 whole, which is shorter than its diff:
```python
import math

import jax
import jax.numpy as jnp
from jax import lax
from jax.experimental import pallas as pl
from jax.experimental.pallas import tpu as pltpu
from jax.sharding import PartitionSpec as P
F32=jnp.float32; BF=jnp.bfloat16
NT=(((1,),(1,)),((),()))
NN=(((1,),(0,)),((),()))
def dot(a,b,dims=NN):
    return lax.dot_general(a,b,dims,preferred_element_type=F32)

def kernel(len_ref, shard_ref, q_ref, up_ref, kvp_ref, kvprev_ref, kvown_ref,
           o_ref, gq_ref, gp_ref, gw_ref,
           k_s, v_s, kt_s, vt_s, bias_s, s_s, w_s, ds_s, gk_s, gv_s):
    dh=128; rows=q_ref.shape[0]; npre=kvp_ref.shape[0]; heads=q_ref.shape[1]//dh
    rb=128; win=rows+rb; nk=npre+win; nresp=len_ref.shape[1]
    scale=dh**-0.5
    c2=scale*math.log2(math.e)
    tot=npre+2*rows
    k_s[0:npre]=kvp_ref[:,0:dh]; v_s[0:npre]=kvp_ref[:,dh:]
    k_s[npre:npre+rows]=kvprev_ref[:,0:dh]; v_s[npre:npre+rows]=kvprev_ref[:,dh:]
    k_s[npre+rows:]=kvown_ref[:,0:dh]; v_s[npre+rows:]=kvown_ref[:,dh:]
    kt_s[...]=k_s[...].T
    vt_s[...]=v_s[...].T
    gk_s[...]=jnp.zeros_like(gk_s); gv_s[...]=jnp.zeros_like(gv_s)
    shard=shard_ref[0]
    def block(i,_):
        r0=pl.multiple_of(i*rb,rb)
        w0=pl.multiple_of(npre+i*rb,rb)
        pos=shard*rows+r0+lax.broadcasted_iota(jnp.int32,(1,rb),1)
        lo=jnp.zeros((1,rb),jnp.int32); end=jnp.int32(0)
        for r in range(nresp):
            end=end+len_ref[0,r]
            lo=jnp.where(pos>=end,end,lo)
        live_row=(pos<end)
        u=(shard-1)*rows+r0+lax.broadcasted_iota(jnp.int32,(win,rb),0)
        bias_s[...]=jnp.where((u>=lo)&(u<=pos),0.0,-jnp.inf).astype(F32)
        def pair(p,_):
            c0=pl.multiple_of(p*2*dh,2*dh)
            q2=q_ref[pl.ds(r0,rb),pl.ds(c0,2*dh)]
            q=jnp.concatenate([q2[:,:dh],q2[:,dh:]],axis=0)
            up2=up_ref[pl.ds(r0,rb),pl.ds(c0,2*dh)]
            up=jnp.concatenate([up2[:,:dh],up2[:,dh:]],axis=0)
            s_s[0:npre]=dot(k_s[0:npre],q,NT)
            s_s[npre:]=dot(k_s[pl.ds(w0,win)],q,NT)
            ch=128
            m=jnp.full((8,2*rb),-jnp.inf,F32)
            for j in range(nk//ch):
                s=s_s[j*ch:(j+1)*ch]*c2
                if j*ch>=npre:
                    b=bias_s[j*ch-npre:(j+1)*ch-npre]
                    s=s+jnp.concatenate([b,b],axis=1)
                s_s[j*ch:(j+1)*ch]=s
                m=jnp.maximum(m,jnp.max(s.reshape(ch//8,8,2*rb),axis=0))
            m=jnp.max(m,axis=0,keepdims=True)
            l=jnp.zeros((8,2*rb),F32)
            for j in range(nk//ch):
                w=jnp.exp2(s_s[j*ch:(j+1)*ch]-m)
                l=l+jnp.sum(w.reshape(ch//8,8,2*rb),axis=0)
                w_s[j*ch:(j+1)*ch]=w.astype(BF)
            l=jnp.sum(l,axis=0,keepdims=True)
            live2=jnp.concatenate([live_row,live_row],axis=1)
            inv=jnp.where(live2,1.0/l,0.0)
            ot=dot(vt_s[:,0:npre],w_s[0:npre])+dot(vt_s[:,pl.ds(w0,win)],w_s[npre:])
            ot=ot*inv
            o=ot.T
            ob=o.astype(BF)
            invc=jnp.broadcast_to(inv,(dh,2*rb)).T
            dof=up.astype(F32)*invc
            dob=dof.astype(BF)
            o_ref[pl.ds(r0,rb),pl.ds(c0,2*dh)]=jnp.concatenate([ob[:rb],ob[rb:]],axis=1)
            prod=(dob.astype(F32)*ob.astype(F32))
            delta=jnp.sum(prod.T,axis=0,keepdims=True)
            s_s[0:npre]=dot(v_s[0:npre],dob,NT)
            s_s[npre:]=dot(v_s[pl.ds(w0,win)],dob,NT)
            for j in range(nk//ch):
                d=w_s[j*ch:(j+1)*ch].astype(F32)*(s_s[j*ch:(j+1)*ch]-delta)
                ds_s[j*ch:(j+1)*ch]=d.astype(BF)
            gqt=(dot(kt_s[:,0:npre],ds_s[0:npre])+dot(kt_s[:,pl.ds(w0,win)],ds_s[npre:]))*scale
            gq=gqt.T.astype(BF)
            gq_ref[pl.ds(r0,rb),pl.ds(c0,2*dh)]=jnp.concatenate([gq[:rb],gq[rb:]],axis=1)
            gk_s[0:npre]+=dot(ds_s[0:npre],q)
            gk_s[pl.ds(w0,win)]+=dot(ds_s[npre:],q)
            gv_s[0:npre]+=dot(w_s[0:npre],dob)
            gv_s[pl.ds(w0,win)]+=dot(w_s[npre:],dob)
            return 0
        lax.fori_loop(0,heads//2,pair,0)
        return 0
    lax.fori_loop(0,rows//rb,block,0)
    gp_ref[:,0:dh]=gk_s[0:npre]*scale
    gp_ref[:,dh:]=gv_s[0:npre]
    gw_ref[:,0:dh]=gk_s[npre:]*scale
    gw_ref[:,dh:]=gv_s[npre:]

def attend(q,up,kvp,kvprev,kvown,lengths,shard):
    rows=q.shape[0]; npre=kvp.shape[0]; dh=128; rb=128; win=rows+rb; nk=npre+win; tot=npre+2*rows
    vm=pl.BlockSpec(memory_space=pltpu.VMEM); sm=pl.BlockSpec(memory_space=pltpu.SMEM)
    sds=jax.ShapeDtypeStruct
    return pl.pallas_call(kernel,
      in_specs=[sm,sm]+[vm]*5, out_specs=[vm]*4,
      out_shape=[sds(q.shape,BF),sds(q.shape,BF),sds((npre,2*dh),F32),sds((2*rows,2*dh),F32)],
      scratch_shapes=[pltpu.VMEM((tot,dh),BF),pltpu.VMEM((tot,dh),BF),pltpu.VMEM((dh,tot),BF),pltpu.VMEM((dh,tot),BF),
         pltpu.VMEM((win,rb),F32),pltpu.VMEM((nk,2*rb),F32),pltpu.VMEM((nk,2*rb),BF),pltpu.VMEM((nk,2*rb),BF),
         pltpu.VMEM((tot,dh),F32),pltpu.VMEM((tot,dh),F32)],
      compiler_params=pltpu.CompilerParams(vmem_limit_bytes=56*2**20),
      name="attend")(lengths,shard,q,up,kvp,kvprev,kvown)


def ring(block, distance):
    size = lax.axis_size("seq")
    return lax.ppermute(block, "seq", [(i, (i + distance) % size) for i in range(size)])


def body(queries, resp_kv, prefix_kv, lengths, upstream):
    rows = queries.shape[1]
    dh = resp_kv.shape[2] // 2
    n_seq = lax.axis_size("seq")
    n_prompt = lax.axis_size("prompt")
    shard = lax.axis_index("seq").astype(jnp.int32)
    part = prefix_kv.shape[1]
    prev = ring(resp_kv[0], 1)
    count = jnp.broadcast_to(jnp.sum(lengths[0]), (8, 128))
    route = [(p * n_seq + s, (p ^ s) * n_seq + s) for p in range(n_prompt) for s in range(n_seq)]
    count = lax.ppermute(count, ("prompt", "seq"), route)
    spread = jnp.broadcast_to(prefix_kv, (n_seq, part, 2 * dh))
    prefix_all = lax.all_to_all(spread, "seq", split_axis=0, concat_axis=0, tiled=True)
    prefix_all = prefix_all.reshape(n_seq * part, 2 * dh)
    attended, grad_query, gp, gw = attend(
        queries[0], upstream[0], prefix_all, prev, resp_kv[0], lengths, shard[None]
    )
    returned = ring(gw[:rows].astype(BF), -1)
    high = (count[0, 0] // 128).astype(BF)
    low = (count[0, 0] % 128).astype(BF)
    tail = jnp.concatenate(
        [jnp.full((n_seq, 16, dh), high, BF), jnp.full((n_seq, 16, dh), low, BF)], axis=2
    )
    packet = jnp.concatenate([gp.astype(BF).reshape(n_seq, part, 2 * dh), tail], axis=1)
    packet = lax.all_to_all(packet, "seq", split_axis=0, concat_axis=0, tiled=True).astype(F32)
    total = jnp.sum(packet[:, part, 0] * 128.0 + packet[:, part, dh])
    factor = jnp.float32(n_prompt * n_seq * rows) / total
    grad_prefix = jnp.sum(packet[:, :part], axis=0) * factor
    grad_resp = (gw[rows:] + returned.astype(F32)) * factor
    grad_query = (grad_query.astype(F32) * factor).astype(BF)
    return (attended[None], grad_query[None], grad_resp[None], grad_prefix[None])


def solution(mesh):
    spec = P("prompt", "seq", None)
    return jax.shard_map(
        body,
        mesh=mesh,
        in_specs=(spec, spec, spec, P("prompt", None), spec),
        out_specs=(spec, spec, spec, spec),
        check_vma=False,
    )
```

time: 204 us -> 86.4 us (0.42); the launches traced: 201 us -> 85.9 us
  blocking collectives: 67.4 us -> 0 us
  matrix products: 42.2 us -> 0 us
  Pallas kernels: 0 us -> 36.5 us
  waiting for transfers between devices: 42.4 us -> 10.8 us
  starting transfers between devices: 6.71 us -> 24.8 us
  local copies, waits for them, and re-layouts: 15.4 us -> 3.58 us
  between operations: 15.9 us -> 4.09 us
  other arithmetic: 11.3 us -> 6.08 us
    unnamed x2 -> x0, waiting for transfers between devices: 42.4 us -> none
    dot_general x48 -> x0, matrix products: 42.2 us -> none  [the longest x8 12.2 us: block_terms(): jnp.einsum('rgk,kd->rgd', dscores, key_part, preferred_element_type=jnp.f...]
    psum x1 -> x0, blocking collectives: 41.1 us -> none  [body(): live_total = lax.psum(jnp.sum(lengths[0]).astype(jnp.float32), 'prompt')]
    pallas_call x0 -> x1, Pallas kernels: none -> 36.5 us  [attend(): pl.pallas_call(kernel, in_specs=[sm, sm] + [vm] * 5, out_specs=[vm] * 4,...]
    all_gather x1 -> x0, blocking collectives: 26.3 us -> none  [body(): prefix_all = lax.all_gather(prefix_kv[0], 'seq', axis=0, tiled=True)]
    all_to_all x0 -> x2, starting transfers between devices: none -> 18 us  [the longest x1 10.7 us: body(): lax.all_to_all(packet, 'seq', split_axis=0, concat_axis=0, tiled=True)]
    unnamed x39 -> x12, local copies, waits for them, and re-layouts: 12.1 us -> 0.83 us
    all_to_all x0 -> x2, waiting for transfers between devices: none -> 9.57 us  [the longest x1 9.56 us: body(): lax.all_to_all(packet, 'seq', split_axis=0, concat_axis=0, tiled=True)]
  transfers between devices with their start and end apart: 3 -> 5, of which waited for: 1 -> 2; matrix products, arithmetic and copies ran while one was open for 11% -> 5% of each run, Pallas kernels for 0% -> 0%
where the time goes in v1:
time: 86.4 us; the launch traced here: 85.9 us
  Pallas kernels  36.5 us (42%)
  starting transfers between devices  24.8 us (29%)
  waiting for transfers between devices  10.8 us (12%)
  other arithmetic  6.08 us (7%)
  between operations  4.09 us (5%)
  local copies, waits for them, and re-layouts  3.58 us (4%)
    pallas_call x1, Pallas kernels, attend(): pl.pallas_call(kernel, in_specs=[sm, sm] + [vm] * 5, out_specs=[vm] * 4,...  36.5 us
    all_to_all x1, starting transfers between devices, body(): lax.all_to_all(packet, 'seq', split_axis=0, concat_axis=0, tiled=True)  10.7 us
    all_to_all x1, waiting for transfers between devices, body(): lax.all_to_all(packet, 'seq', split_axis=0, concat_axis=0, tiled=True)  9.56 us
    all_to_all x1, starting transfers between devices, body(): lax.all_to_all(spread, 'seq', split_axis=0, concat_axis=0, tiled=True)  7.34 us
    ppermute x1, starting transfers between devices, body(): count = lax.ppermute(count, ('prompt', 'seq'), route)  4.9 us
    ppermute x2, starting transfers between devices, ring(): lax.ppermute(block, 'seq', [(i, (i + distance) % size) for i in range(siz...  1.89 us
  transfers between devices with their start and end apart: 5, of which 2 were waited for; matrix products, arithmetic and copies ran while one was open for 5% of the time, Pallas kernels for 0%

profile of v1, /device:TPU:1, one launch (start us, length us, event | category | flops | bytes accessed | tf_op | source)
XLA Modules:
  0.0 85.9 jit_solution(16626504446311244976)
XLA Ops:
  0.6 0.0 copy-start.3
  0.6 0.0 copy-start.5
  0.7 1.5 %broadcast_in_dim.29 = bf16[16,48,256]{2,1,0:T(8,128)(2,1)} broadcast(bf16[48,256]{1,0:T(8,128)(2,1)} %bitcast.21), dimensions={1,2} | broadcast | bytes 417792 | tf_op jit(solution)/shard_map/broadcast_in_dim | solution.py:128
  2.2 7.3 %all-to-all-start = ((bf16[16,48,256]{2,1,0:T(8,128)(2,1)}), bf16[16,48,256]{2,1,0:T(8,128)(2,1)S(1)}, u32[]{:S(2)}, u32[]{:S(2)}) async-start(bf16[16,48,256]{2,1,0:T(8,128)(2,1)} %broadcast_in_dim.29), calls=%async_computation | async-start | bytes 786432 | tf_op jit(solution)/shard_map/all_to_all | solution.py:129
  9.5 0.0 copy-done.3
  9.5 1.7 %collective-permute-start = (bf16[512,256]{1,0:T(8,128)(2,1)S(1)}, bf16[512,256]{1,0:T(8,128)(2,1)S(1)}, u32[]{:S(2)}, u32[]{:S(2)}) collective-permute-start(bf16[512,256]{1,0:T(8,128)(2,1)S(1)} %bitcast.20), channel_id=1, source_target_pairs={{0,1},{1,2},{2,3},{3,4},{4,5},{5,6},{6,7},{7,8},{8,9},{9,10},{10,1... | collective-permute-start | bytes 786440 | tf_op jit(solution)/shard_map/ppermute | solution.py:114
  11.3 0.0 copy-done.5
  11.3 0.6 reduce_sum.27
  11.9 0.6 broadcast_in_dim.31
  12.5 4.9 %collective-permute-start.1 = (s32[8,128]{1,0:T(8,128)S(1)}, s32[8,128]{1,0:T(8,128)S(1)}, u32[]{:S(2)}, u32[]{:S(2)}) collective-permute-start(s32[8,128]{1,0:T(8,128)S(1)} %broadcast_in_dim.31), channel_id=1, source_target_pairs={{0,0},{1,17},{2,34},{3,51},{4,68},{5,85},{6,102},{7,119},{8,136},{... | collective-permute-start | bytes 12296 | tf_op jit(solution)/shard_map/ppermute | solution.py:127
  17.5 1.3 %collective-permute-done.1 = s32[8,128]{1,0:T(8,128)S(1)} collective-permute-done((s32[8,128]{1,0:T(8,128)S(1)}, s32[8,128]{1,0:T(8,128)S(1)}, u32[]{:S(2)}, u32[]{:S(2)}) %collective-permute-start.1) | collective-permute-done | bytes 4128 | tf_op jit(solution)/shard_map/ppermute | solution.py:127
  18.7 0.5 slice.20
  21.9 0.0 collective-permute-done.kvprev_ref
  21.9 0.0 copy-start.4
  21.9 0.0 all-to-all-done
  21.9 0.0 copy-start
  21.9 0.7 copy-done.4
  22.6 0.1 copy-done
  22.7 36.5 %attend.1 = (bf16[512,1024]{1,0:T(8,128)(2,1)}, bf16[512,1024]{1,0:T(8,128)(2,1)}, f32[768,256]{1,0:T(8,128)}, f32[1024,256]{1,0:T(8,128)}) custom-call(s32[1,16]{1,0:T(1,128)} %len_ref.1, s32[1]{0:T(128)} %bitcast.shard_ref, bf16[512,1024]{1,0:T(8,128)(2,1)} %bitcast.17, bf16[512,1024]{1,0:T(8,128)(2,1)} %bitcast.18, bf16[768,256]{1,0:T(8,128)(2,1)} %bitcast.16, ...), custom_call_target="tpu_custom_call" | custom-call | tf_op jit(solution)/shard_map/attend/pallas_call | solution.py:102
  59.2 1.2 %convert_element_type.23 = bf16[768,256]{1,0:T(8,128)(2,1)S(1)} convert(f32[768,256]{1,0:T(8,128)} %get-tuple-element.10) | non-fusion elementwise | flops 196608 | bytes 1179648 | tf_op jit(solution)/shard_map/convert_element_type | solution.py:140
  60.4 0.0 copy-start.2
  60.4 0.8 pad_maximum_fusion
  61.3 10.7 %all-to-all-start.1 = ((bf16[16,64,256]{2,1,0:T(8,128)(2,1)}), bf16[16,64,256]{2,1,0:T(8,128)(2,1)S(1)}, u32[]{:S(2)}, u32[]{:S(2)}) async-start(bf16[16,64,256]{2,1,0:T(8,128)(2,1)} %pad_maximum_fusion), calls=%async_computation.1 | async-start | bytes 1048576 | tf_op jit(solution)/shard_map/all_to_all | solution.py:141
  72.0 0.0 copy-done.2
  72.0 0.0 copy-start.1
  72.0 0.2 collective-permute-start.2
  72.2 9.6 %all-to-all-done.1 = bf16[16,64,256]{2,1,0:T(8,128)(2,1)S(1)} async-done(((bf16[16,64,256]{2,1,0:T(8,128)(2,1)}), bf16[16,64,256]{2,1,0:T(8,128)(2,1)S(1)}, u32[]{:S(2)}, u32[]{:S(2)}) %all-to-all-start.1) | async-done | bytes 524320 | tf_op jit(solution)/shard_map/all_to_all | solution.py:141
  81.8 0.1 convert_element_type.26
  81.9 0.1 slice_reduce_fusion
  82.0 0.6 fusion.1
  83.3 0.6 multiply_bitcast_fusion.1
  83.9 0.0 copy-done.1
  83.9 1.2 %fusion = bf16[1,512,1024]{2,1,0:T(8,128)(2,1)} fusion(bf16[512,1024]{1,0:T(8,128)(2,1)S(1)} %copy-done.1, f32[]{:T(128)S(6)} %div.14), kind=kLoop, calls=%fused_computation.1 | loop fusion | flops 1572864 | bytes 2097156 | tf_op jit(solution)/shard_map/broadcast_in_dim | solution.py:147
  85.1 0.0 collective-permute-done.2
  85.1 0.8 multiply_bitcast_fusion
  (4 shorter events, 0.1 us)
Async XLA Ops:
  0.6 8.9 %copy-start.3 = (bf16[1,512,256]{2,1,0:T(8,128)(2,1)S(1)}, bf16[1,512,256]{2,1,0:T(8,128)(2,1)}, u32[]{:S(2)}) copy-start(bf16[1,512,256]{2,1,0:T(8,128)(2,1)} %param.6) | copy-start | bytes 786436
  0.6 10.6 %copy-start.5 = (s32[1,16]{1,0:T(1,128)S(1)}, s32[1,16]{1,0:T(1,128)}, u32[]{:S(2)}) copy-start(s32[1,16]{1,0:T(1,128)} %len_ref.1) | copy-start | bytes 196
  2.2 19.7 %all-to-all-start = ((bf16[16,48,256]{2,1,0:T(8,128)(2,1)}), bf16[16,48,256]{2,1,0:T(8,128)(2,1)S(1)}, u32[]{:S(2)}, u32[]{:S(2)}) async-start(bf16[16,48,256]{2,1,0:T(8,128)(2,1)} %broadcast_in_dim.29), calls=%async_computation | async-start | bytes 786432 | tf_op jit(solution)/shard_map/all_to_all | solution.py:129
  9.5 12.3 %collective-permute-start = (bf16[512,256]{1,0:T(8,128)(2,1)S(1)}, bf16[512,256]{1,0:T(8,128)(2,1)S(1)}, u32[]{:S(2)}, u32[]{:S(2)}) collective-permute-start(bf16[512,256]{1,0:T(8,128)(2,1)S(1)} %bitcast.20), channel_id=1, source_target_pairs={{0,1},{1,2},{2,3},{3,4},{4,5},{5,6},{6,7},{7,8},{8,9},{9,10},{10,1... | collective-permute-start | bytes 786440 | tf_op jit(solution)/shard_map/ppermute | solution.py:114
  12.5 6.2 %collective-permute-start.1 = (s32[8,128]{1,0:T(8,128)S(1)}, s32[8,128]{1,0:T(8,128)S(1)}, u32[]{:S(2)}, u32[]{:S(2)}) collective-permute-start(s32[8,128]{1,0:T(8,128)S(1)} %broadcast_in_dim.31), channel_id=1, source_target_pairs={{0,0},{1,17},{2,34},{3,51},{4,68},{5,85},{6,102},{7,119},{8,136},{... | collective-permute-start | bytes 12296 | tf_op jit(solution)/shard_map/ppermute | solution.py:127
  21.9 0.7 copy-start.4
  21.9 0.8 copy-start
  60.4 11.6 %copy-start.2 = (f32[1024,256]{1,0:T(8,128)S(1)}, f32[1024,256]{1,0:T(8,128)}, u32[]{:S(2)}) copy-start(f32[1024,256]{1,0:T(8,128)} %get-tuple-element.11) | copy-start | bytes 3145732
  61.3 20.5 %all-to-all-start.1 = ((bf16[16,64,256]{2,1,0:T(8,128)(2,1)}), bf16[16,64,256]{2,1,0:T(8,128)(2,1)S(1)}, u32[]{:S(2)}, u32[]{:S(2)}) async-start(bf16[16,64,256]{2,1,0:T(8,128)(2,1)} %pad_maximum_fusion), calls=%async_computation.1 | async-start | bytes 1048576 | tf_op jit(solution)/shard_map/all_to_all | solution.py:141
  72.0 11.9 %copy-start.1 = (bf16[512,1024]{1,0:T(8,128)(2,1)S(1)}, bf16[512,1024]{1,0:T(8,128)(2,1)}, u32[]{:S(2)}) copy-start(bf16[512,1024]{1,0:T(8,128)(2,1)} %get-tuple-element.9) | copy-start | bytes 3145732
  72.0 13.0 %collective-permute-start.2 = (bf16[512,256]{1,0:T(8,128)(2,1)S(1)}, bf16[512,256]{1,0:T(8,128)(2,1)S(1)}, u32[]{:S(2)}, u32[]{:S(2)}) collective-permute-start(bf16[512,256]{1,0:T(8,128)(2,1)S(1)} %slice.41), channel_id=1, source_target_pairs={{0,15},{1,0},{2,1},{3,2},{4,3},{5,4},{6,5},{7,6},{8,7},{9,8},{10,9... | collective-permute-start | bytes 786440 | tf_op jit(solution)/shard_map/ppermute | solution.py:114

commit v2 on v1

v2 whole, which is shorter than its diff:
```python
import functools
import math

import jax
import jax.numpy as jnp
from jax import lax
from jax.experimental import pallas as pl
from jax.experimental.pallas import tpu as pltpu
from jax.sharding import PartitionSpec as P

F32 = jnp.float32
BF = jnp.bfloat16
NN = (((1,), (0,)), ((), ()))
NT = (((1,), (1,)), ((), ()))
DH = 128
RB = 128
CH = 64
BLOCK = 1408
SCALE = DH**-0.5
LOG2_SCALE = SCALE * math.log2(math.e)


def dot(a, b, dims=NN):
    return lax.dot_general(a, b, dims, preferred_element_type=F32)


def tile(p):
    return slice(p * 2 * RB, (p + 1) * 2 * RB)


def stack_heads(pair):
    return jnp.concatenate([pair[:, :DH], pair[:, DH:]], axis=0)


def unstack_heads(rows):
    return jnp.concatenate([rows[:RB], rows[RB:]], axis=1)


def first_slots(len_ref, first, width):
    pos = first + lax.broadcasted_iota(jnp.int32, (1, width), 1)
    start = jnp.zeros((1, width), jnp.int32)
    end = jnp.int32(0)
    for r in range(len_ref.shape[1]):
        end = end + len_ref[0, r]
        start = jnp.where(pos >= end, end, start)
    return pos, start, pos < end


def row_total(values):
    return jnp.sum(values.reshape(values.shape[0] // 8, 8, values.shape[1]), axis=0)


def row_peak(values):
    return jnp.max(values.reshape(values.shape[0] // 8, 8, values.shape[1]), axis=0)


def interleave(*streams):
    pieces = [list(stream) for stream in streams]
    longest = max(len(items) for items in pieces)
    for i in range(longest):
        for items in pieces:
            for piece in items[i * len(items) // longest : (i + 1) * len(items) // longest]:
                piece()


def attend(len_ref, shard_ref, q_ref, up_ref, kv_ref, prev_ref, own_ref,
           o_ref, gq_ref, packet_ref, gprev_ref, gown_ref,
           k_s, v_s, kt_s, vt_s, bias_s, s_s, t_s, w_s, ds_s, q_s, d_s, gk_s, gv_s):
    rows = prev_ref.shape[0]
    prefix = kv_ref.shape[0]
    win = rows + RB
    n = prefix + win
    tiles = q_ref.shape[1] // (2 * DH)
    step = pl.program_id(0)

    @pl.when(step == 0)
    def _():
        for ref, low in ((kv_ref, 0), (prev_ref, prefix), (own_ref, prefix + rows)):
            high = low + ref.shape[0]
            k_s[low:high] = ref[:, :DH]
            v_s[low:high] = ref[:, DH:]
            kt_s[:, low:high] = ref[:, :DH].T
            vt_s[:, low:high] = ref[:, DH:].T
        gk_s[...] = jnp.zeros_like(gk_s)
        gv_s[...] = jnp.zeros_like(gv_s)

    first = shard_ref[0] * rows + step * RB
    pos, start, live = first_slots(len_ref, first, RB)
    live = jnp.concatenate([live, live], axis=1)
    slot = first - rows + lax.broadcasted_iota(jnp.int32, (win, RB), 0)
    bias_s[...] = jnp.where((slot >= start) & (slot <= pos), 0.0, -jnp.inf).astype(F32)
    span = pl.ds(pl.multiple_of(prefix + step * RB, RB), win)
    peak, part, inv, delta = {}, {}, {}, {}

    def key_blocks(size):
        for j in range(0, prefix, size):
            block = slice(j, min(j + size, prefix))
            yield block, block
        for j in range(0, win, size):
            high = min(j + size, win)
            whole = pl.ds(pl.multiple_of(prefix + step * RB + j, RB), high - j)
            yield slice(prefix + j, prefix + high), whole

    def scores(p):
        def piece(here, there):
            s_s[here, tile(p)] = dot(k_s[there], q_s[tile(p)], NT)

        def stack():
            q_s[tile(p)] = stack_heads(q_ref[:, tile(p)])

        return [stack] + [functools.partial(piece, *block) for block in key_blocks(BLOCK)]

    def peaks(p):
        def piece(j):
            s = s_s[j : j + CH, tile(p)] * LOG2_SCALE
            if j >= prefix:
                b = bias_s[j - prefix : j - prefix + CH]
                s = s + jnp.concatenate([b, b], axis=1)
            s_s[j : j + CH, tile(p)] = s
            top = row_peak(s)
            peak[p] = jnp.maximum(peak[p], top) if j else top

        def final():
            peak[p] = jnp.max(peak[p], axis=0, keepdims=True)

        return [functools.partial(piece, j) for j in range(0, n, CH)] + [final]

    def weigh(p):
        def piece(j):
            w = jnp.exp2(s_s[j : j + CH, tile(p)] - peak[p])
            part[p] = part[p] + row_total(w) if j else row_total(w)
            w_s[j : j + CH, tile(p)] = w.astype(BF)

        def final():
            inv[p] = jnp.where(live, 1.0 / jnp.sum(part[p], axis=0, keepdims=True), 0.0)
            spread = jnp.broadcast_to(inv[p], (DH, 2 * RB)).T
            d_s[tile(p)] = (stack_heads(up_ref[:, tile(p)]).astype(F32) * spread).astype(BF)

        return [functools.partial(piece, j) for j in range(0, n, CH)] + [final]

    def mix(p):
        def piece():
            ot = dot(vt_s[:, :prefix], w_s[:prefix, tile(p)]) + dot(vt_s[:, span], w_s[prefix:, tile(p)])
            o = (ot * inv[p]).T.astype(BF)
            o_ref[:, tile(p)] = unstack_heads(o)
            product = d_s[tile(p)].astype(F32) * o.astype(F32)
            delta[p] = jnp.sum(product.T, axis=0, keepdims=True)

        return [piece]

    def slopes(p):
        def piece(here, there):
            t_s[here, tile(p)] = dot(v_s[there], d_s[tile(p)], NT)

        return [functools.partial(piece, *block) for block in key_blocks(BLOCK)]

    def score_grads(p):
        def piece(j):
            w = w_s[j : j + CH, tile(p)].astype(F32)
            ds_s[j : j + CH, tile(p)] = (w * (t_s[j : j + CH, tile(p)] - delta[p])).astype(BF)

        return [functools.partial(piece, j) for j in range(0, n, CH)]

    def key_sums(total_s, left_s, right_s):
        def piece(here, there):
            total_s[there] += dot(left_s[here], right_s[...])

        return [functools.partial(piece, *block) for block in key_blocks(BLOCK)]

    def query_grads(p):
        def piece():
            gqt = dot(kt_s[:, :prefix], ds_s[:prefix, tile(p)]) + dot(kt_s[:, span], ds_s[prefix:, tile(p)])
            gq_ref[:, tile(p)] = unstack_heads((gqt * SCALE).T.astype(BF))

        return [piece]

    for stage in (scores, peaks, weigh, mix, slopes, score_grads):
        for p in range(tiles):
            interleave(stage(p))
    interleave(key_sums(gv_s, w_s, d_s))
    for p in range(tiles):
        interleave(query_grads(p))
    interleave(key_sums(gk_s, ds_s, q_s))

    @pl.when(step == pl.num_programs(0) - 1)
    def _():
        gprev_ref[:, :DH] = (gk_s[prefix : prefix + rows] * SCALE).astype(BF)
        gprev_ref[:, DH:] = gv_s[prefix : prefix + rows].astype(BF)
        gown_ref[:, :DH] = gk_s[prefix + rows :] * SCALE
        gown_ref[:, DH:] = gv_s[prefix + rows :]
        parts, each, _ = packet_ref.shape
        for i in range(parts):
            own = slice(i * each, (i + 1) * each)
            packet_ref[i, :, :DH] = (gk_s[own] * SCALE).astype(BF)
            packet_ref[i, :, DH:] = gv_s[own].astype(BF)


def call(kernel, name, steps, in_specs, outs, scratch, flops, traffic):
    return pl.pallas_call(
        kernel,
        name=name,
        grid=(steps,),
        in_specs=in_specs,
        out_specs=[spec for spec, _ in outs],
        out_shape=[shape for _, shape in outs],
        scratch_shapes=[pltpu.VMEM(shape, dtype) for shape, dtype in scratch],
        compiler_params=pltpu.CompilerParams(
            dimension_semantics=("arbitrary",), vmem_limit_bytes=56 * 2**20
        ),
        cost_estimate=pl.CostEstimate(flops=flops, bytes_accessed=traffic, transcendentals=0),
    )


def kernels(rows, prefix, heads, parts):
    steps = rows // RB
    cols = heads * RB
    win = rows + RB
    small = pl.BlockSpec(memory_space=pltpu.SMEM)
    row_spec = pl.BlockSpec((RB, heads * DH), lambda i: (i, 0))
    whole = lambda *shape: pl.BlockSpec(shape, lambda i: (0,) * len(shape))
    kv_spec = whole(rows, 2 * DH)
    sds = jax.ShapeDtypeStruct
    row_out = (row_spec, sds((rows, heads * DH), BF))
    packet = (parts, prefix // parts, 2 * DH)
    n = prefix + win
    every = prefix + 2 * rows
    return call(
        attend, "attend", steps,
        [small, small, row_spec, row_spec, whole(prefix, 2 * DH), kv_spec, kv_spec],
        [row_out, row_out, (whole(*packet), sds(packet, BF)),
         (kv_spec, sds((rows, 2 * DH), BF)), (kv_spec, sds((rows, 2 * DH), F32))],
        [((every, DH), BF), ((every, DH), BF), ((DH, every), BF), ((DH, every), BF), ((win, RB), F32),
         ((n, cols), F32), ((n, cols), F32), ((n, cols), BF), ((n, cols), BF),
         ((cols, DH), BF), ((cols, DH), BF), ((every, DH), F32), ((every, DH), F32)],
        12 * rows * heads * DH * n, 6 * 2**20,
    )


def ring(block, distance):
    size = lax.axis_size("seq")
    return lax.ppermute(block, "seq", [(i, (i + distance) % size) for i in range(size)])


def exchange(packets):
    return lax.all_to_all(packets, "seq", split_axis=0, concat_axis=0, tiled=True)


def pair_routes(n_prompt):
    side = math.isqrt(n_prompt)

    def paired(k, odd):
        return ((k + odd) ^ 1) - odd

    for odd in (0, 1):
        yield [(p, (paired(p // side, odd) % side) * side + p % side) for p in range(n_prompt)]
    for odd in (0, 1):
        yield [(p, p // side * side + paired(p % side, odd) % side) for p in range(n_prompt)]


def body(queries, resp_kv, prefix_kv, lengths, upstream):
    rows, width = queries.shape[1:]
    n_seq = lax.axis_size("seq")
    n_prompt = lax.axis_size("prompt")
    shard = lax.axis_index("seq").astype(jnp.int32)[None]
    part = prefix_kv.shape[1]
    core = kernels(rows, n_seq * part, width // DH, n_seq)
    first, second, third, fourth = pair_routes(n_prompt)
    counts = lengths
    counts = counts + lax.ppermute(counts, "prompt", first)
    prev = ring(resp_kv[0], 1)
    prefix_all = exchange(jnp.broadcast_to(prefix_kv, (n_seq, part, 2 * DH)))
    prefix_all = prefix_all.reshape(n_seq * part, 2 * DH)
    counts = counts + lax.ppermute(counts, "prompt", second)
    incoming = lax.ppermute(counts, "prompt", third)
    attended, grad_query, packet, g_prev, g_own = core(
        lengths, shard, queries[0], upstream[0], prefix_all, prev, resp_kv[0]
    )
    packet, incoming = lax.optimization_barrier((packet, incoming))
    packet = exchange(packet)
    returned = ring(g_prev, -1)
    counts = counts + incoming
    counts = counts + lax.ppermute(counts, "prompt", fourth)
    factor = jnp.float32(n_prompt * n_seq * rows) / jnp.sum(counts).astype(F32)
    grad_query = (grad_query.astype(F32) * factor).astype(BF)
    grad_prefix = jnp.sum(packet.astype(F32), axis=0) * factor
    grad_resp = (g_own + returned.astype(F32)) * factor
    return (attended[None], grad_query[None], grad_resp[None], grad_prefix[None])


def solution(mesh):
    spec = P("prompt", "seq", None)
    return jax.shard_map(
        body,
        mesh=mesh,
        in_specs=(spec, spec, spec, P("prompt", None), spec),
        out_specs=(spec, spec, spec, spec),
        check_vma=False,
    )
```

time: 86.4 us -> 65.7 us (0.76)
  Pallas kernels: 36.5 us -> 23.7 us
  waiting for transfers between devices: 10.8 us -> 7.07 us
  between operations: 4.09 us -> 1.39 us
  other arithmetic: 6.08 us -> 4.64 us
  starting transfers between devices: 24.8 us -> 26.2 us
  local copies, waits for them, and re-layouts: 3.58 us -> 2.4 us
    pallas_call x1, Pallas kernels: 36.5 us -> 23.7 us  [body(): core(lengths, shard, queries[0], upstream[0], prefix_all, prev, resp_kv[0])]
    all_to_all x2, waiting for transfers between devices: 9.57 us -> 0.01 us  [exchange(): lax.all_to_all(packets, 'seq', split_axis=0, concat_axis=0, tiled=True)]
    ppermute x1 -> x4, waiting for transfers between devices: 1.27 us -> 7.06 us  [the longest x1 4.46 us: body(): counts = counts + lax.ppermute(counts, 'prompt', fourth)]
    ppermute x1 -> x4, starting transfers between devices: 4.9 us -> 10.1 us  [the longest x1 3.39 us: body(): counts = counts + lax.ppermute(counts, 'prompt', fourth)]
    all_to_all x2, starting transfers between devices: 18 us -> 13.9 us  [exchange(): lax.all_to_all(packets, 'seq', split_axis=0, concat_axis=0, tiled=True)]
    broadcast_in_dim x1, other arithmetic: 1.18 us -> 2.47 us  [body(): grad_query[None]]
    convert_element_type x2 -> x0, other arithmetic: 1.28 us -> none  [the longest x1 1.17 us: body(): gp.astype(BF).reshape(n_seq, part, 2 * dh)]
    broadcast_in_dim x3 -> x1, local copies, waits for them, and re-layouts: 2.2 us -> 1.55 us  [body(): prefix_all = exchange(jnp.broadcast_to(prefix_kv, (n_seq, part, 2 * DH)))]
  transfers between devices with their start and end apart: 5 -> 8, of which waited for: 2 -> 3; matrix products, arithmetic and copies ran while one was open for 5% -> 6% of each run, Pallas kernels for 0% -> 36%
where the time goes in v2:
time: 65.7 us; the launch traced here: 65.3 us
  starting transfers between devices  26.2 us (40%)
  Pallas kernels  23.7 us (36%)
  waiting for transfers between devices  7.07 us (11%)
  other arithmetic  4.64 us (7%)
  local copies, waits for them, and re-layouts  2.4 us (4%)
  between operations  1.39 us (2%)
    pallas_call x1, Pallas kernels, body(): core(lengths, shard, queries[0], upstream[0], prefix_all, prev, resp_kv[0])  23.7 us
    all_to_all x2, starting transfers between devices, exchange(): lax.all_to_all(packets, 'seq', split_axis=0, concat_axis=0, tiled=True)  13.9 us
    ppermute x1, waiting for transfers between devices, body(): counts = counts + lax.ppermute(counts, 'prompt', fourth)  4.46 us
    ppermute x1, starting transfers between devices, body(): counts = counts + lax.ppermute(counts, 'prompt', fourth)  3.39 us
    ppermute x1, starting transfers between devices, body(): incoming = lax.ppermute(counts, 'prompt', third)  2.99 us
    ppermute x1, starting transfers between devices, body(): counts = counts + lax.ppermute(counts, 'prompt', second)  2.48 us
    broadcast_in_dim x1, other arithmetic, body(): grad_query[None]  2.47 us
    ppermute x2, starting transfers between devices, ring(): lax.ppermute(block, 'seq', [(i, (i + distance) % size) for i in range(siz...  2.2 us
  transfers between devices with their start and end apart: 8, of which 3 were waited for; matrix products, arithmetic and copies ran while one was open for 6% of the time, Pallas kernels for 36%

profile of v2, /device:TPU:1, one launch (start us, length us, event | category | flops | bytes accessed | tf_op | source)
XLA Modules:
  0.0 65.3 jit_solution(4774795644374396453)
XLA Ops:
  0.6 0.0 copy-start.2
  0.6 0.0 copy-start.4
  0.7 1.5 %broadcast_in_dim.22 = bf16[16,48,256]{2,1,0:T(8,128)(2,1)} broadcast(bf16[48,256]{1,0:T(8,128)(2,1)} %bitcast.14), dimensions={1,2} | broadcast | bytes 417792 | tf_op jit(solution)/shard_map/broadcast_in_dim | solution.py:271
  2.2 7.3 %all-to-all-start = ((bf16[16,48,256]{2,1,0:T(8,128)(2,1)}), bf16[16,48,256]{2,1,0:T(8,128)(2,1)S(1)}, u32[]{:S(2)}, u32[]{:S(2)}) async-start(bf16[16,48,256]{2,1,0:T(8,128)(2,1)} %broadcast_in_dim.22), calls=%async_computation | async-start | bytes 786432 | tf_op jit(solution)/shard_map/all_to_all | solution.py:245
  9.5 0.0 copy-done.2
  9.5 1.7 %collective-permute-start = (bf16[512,256]{1,0:T(8,128)(2,1)S(1)}, bf16[512,256]{1,0:T(8,128)(2,1)S(1)}, u32[]{:S(2)}, u32[]{:S(2)}) collective-permute-start(bf16[512,256]{1,0:T(8,128)(2,1)S(1)} %bitcast.18), channel_id=1, source_target_pairs={{0,1},{1,2},{2,3},{3,4},{4,5},{5,6},{6,7},{7,8},{8,9},{9,10},{10,1... | collective-permute-start | bytes 786440 | tf_op jit(solution)/shard_map/ppermute | solution.py:241
  11.3 0.0 copy-done.4
  11.3 1.2 %collective-permute-start.1 = (s32[1,16]{1,0:T(1,128)S(1)}, s32[1,16]{1,0:T(1,128)S(1)}, u32[]{:S(2)}, u32[]{:S(2)}) collective-permute-start(s32[1,16]{1,0:T(1,128)S(1)} %copy-done.4), channel_id=1, source_target_pairs={{0,64},{16,80},{32,96},{48,112},{64,0},{80,16},{96,32},{112,48},{1... | collective-permute-start | bytes 200 | tf_op jit(solution)/shard_map/ppermute | solution.py:269
  12.5 1.5 %collective-permute-done.1 = s32[1,16]{1,0:T(1,128)S(1)} collective-permute-done((s32[1,16]{1,0:T(1,128)S(1)}, s32[1,16]{1,0:T(1,128)S(1)}, u32[]{:S(2)}, u32[]{:S(2)}) %collective-permute-start.1) | collective-permute-done | bytes 96 | tf_op jit(solution)/shard_map/ppermute | solution.py:269
  14.0 2.5 %collective-permute-start.2 = (s32[1,16]{1,0:T(1,128)S(1)}, s32[1,16]{1,0:T(1,128)S(1)}, u32[]{:S(2)}, u32[]{:S(2)}) collective-permute-start(s32[1,16]{1,0:T(1,128)S(1)} %add.15), channel_id=1, source_target_pairs={{0,192},{16,208},{32,224},{48,240},{64,128},{80,144},{96,160},{112... | collective-permute-start | bytes 200 | tf_op jit(solution)/shard_map/ppermute | solution.py:273
  16.4 1.1 %collective-permute-done.2 = s32[1,16]{1,0:T(1,128)S(1)} collective-permute-done((s32[1,16]{1,0:T(1,128)S(1)}, s32[1,16]{1,0:T(1,128)S(1)}, u32[]{:S(2)}, u32[]{:S(2)}) %collective-permute-start.2) | collective-permute-done | bytes 96 | tf_op jit(solution)/shard_map/ppermute | solution.py:273
  17.6 3.0 %collective-permute-start.3 = (s32[1,16]{1,0:T(1,128)S(1)}, s32[1,16]{1,0:T(1,128)S(1)}, u32[]{:S(2)}, u32[]{:S(2)}) collective-permute-start(s32[1,16]{1,0:T(1,128)S(1)} %add.16), channel_id=1, source_target_pairs={{0,16},{16,0},{32,48},{48,32},{64,80},{80,64},{96,112},{112,96},{1... | collective-permute-start | bytes 200 | tf_op jit(solution)/shard_map/ppermute | solution.py:274
  20.5 0.0 collective-permute-done.prev_ref
  20.6 0.0 copy-start.3
  20.6 0.0 all-to-all-done
  20.6 0.0 copy-start.1
  20.6 0.7 %copy-done.3 = bf16[512,256]{1,0:T(8,128)(2,1)} copy-done((bf16[512,256]{1,0:T(8,128)(2,1)}, bf16[512,256]{1,0:T(8,128)(2,1)S(1)}, u32[]{:S(2)}) %copy-start.3) | copy-done | bytes 262168
  21.2 0.2 copy-done.1
  21.4 23.7 %attend.1 = (bf16[512,1024]{1,0:T(8,128)(2,1)}, bf16[512,1024]{1,0:T(8,128)(2,1)}, bf16[16,48,256]{2,1,0:T(8,128)(2,1)}, bf16[512,256]{1,0:T(8,128)(2,1)}, f32[512,256]{1,0:T(8,128)}) custom-call(s32[1,16]{1,0:T(1,128)} %len_ref.1, s32[1]{0:T(128)} %bitcast.shard_ref, bf16[512,1024]{1,0:T(8,128)(2,1)} %bitcast.15, bf16[512,1024]{1,0:T(8,128)(2,1)} %bitcast.16, ...), custom_call_target="tpu_custom_call" | custom-call | flops 8858370048 | bytes 6291456 | tf_op jit(solution)/shard_map/attend/pallas_call | solution.py:275
  45.1 0.0 collective-permute-done.3
  45.1 6.5 %all-to-all-start.1 = ((bf16[16,48,256]{2,1,0:T(8,128)(2,1)}), bf16[16,48,256]{2,1,0:T(8,128)(2,1)S(1)}, u32[]{:S(2)}, u32[]{:S(2)}) async-start(bf16[16,48,256]{2,1,0:T(8,128)(2,1)} %get-tuple-element.17), calls=%async_computation.1 | async-start | bytes 786432 | tf_op jit(solution)/shard_map/all_to_all | solution.py:245
  51.6 3.4 %collective-permute-start.4 = (s32[1,16]{1,0:T(1,128)S(1)}, s32[1,16]{1,0:T(1,128)S(1)}, u32[]{:S(2)}, u32[]{:S(2)}) collective-permute-start(s32[1,16]{1,0:T(1,128)S(1)} %add.17), channel_id=1, source_target_pairs={{0,48},{16,32},{32,16},{48,0},{64,112},{80,96},{96,80},{112,64},{1... | collective-permute-start | bytes 200 | tf_op jit(solution)/shard_map/ppermute | solution.py:282
  55.0 0.5 collective-permute-start.5
  55.5 4.5 %collective-permute-done.4 = s32[1,16]{1,0:T(1,128)S(1)} collective-permute-done((s32[1,16]{1,0:T(1,128)S(1)}, s32[1,16]{1,0:T(1,128)S(1)}, u32[]{:S(2)}, u32[]{:S(2)}) %collective-permute-start.4) | collective-permute-done | bytes 96 | tf_op jit(solution)/shard_map/ppermute | solution.py:282
  60.0 0.6 add_reduce_fusion
  61.3 0.0 copy-start
  61.3 2.5 %fusion = bf16[1,512,1024]{2,1,0:T(8,128)(2,1)} fusion(bf16[512,1024]{1,0:T(8,128)(2,1)} %get-tuple-element.12, f32[]{:T(128)S(6)} %div.3), kind=kLoop, calls=%fused_computation.1 | loop fusion | flops 1572864 | bytes 2097156 | tf_op jit(solution)/shard_map/broadcast_in_dim | solution.py:287
  63.8 0.0 collective-permute-done.5
  63.8 0.0 copy-done
  63.8 0.8 %multiply_bitcast_fusion = f32[1,512,256]{2,1,0:T(8,128)} fusion(f32[512,256]{1,0:T(8,128)S(1)} %copy-done, bf16[512,256]{1,0:T(8,128)(2,1)S(1)} %collective-permute-done.5, f32[]{:T(128)S(6)} %div.3), kind=kLoop, calls=%fused_computation.3 | loop fusion | flops 393216 | bytes 1310724 | tf_op jit(solution)/shard_map/broadcast_in_dim | solution.py:287
  64.7 0.0 all-to-all-done.1
  64.7 0.1 convert_reduce_fusion
  64.7 0.6 multiply_bitcast_fusion.1
  (3 shorter events, 0.0 us)
Async XLA Ops:
  0.6 8.9 %copy-start.2 = (bf16[1,512,256]{2,1,0:T(8,128)(2,1)S(1)}, bf16[1,512,256]{2,1,0:T(8,128)(2,1)}, u32[]{:S(2)}) copy-start(bf16[1,512,256]{2,1,0:T(8,128)(2,1)} %param.6) | copy-start | bytes 786436
  0.6 10.6 %copy-start.4 = (s32[1,16]{1,0:T(1,128)S(1)}, s32[1,16]{1,0:T(1,128)}, u32[]{:S(2)}) copy-start(s32[1,16]{1,0:T(1,128)} %len_ref.1) | copy-start | bytes 196
  2.2 18.4 %all-to-all-start = ((bf16[16,48,256]{2,1,0:T(8,128)(2,1)}), bf16[16,48,256]{2,1,0:T(8,128)(2,1)S(1)}, u32[]{:S(2)}, u32[]{:S(2)}) async-start(bf16[16,48,256]{2,1,0:T(8,128)(2,1)} %broadcast_in_dim.22), calls=%async_computation | async-start | bytes 786432 | tf_op jit(solution)/shard_map/all_to_all | solution.py:245
  9.5 11.0 %collective-permute-start = (bf16[512,256]{1,0:T(8,128)(2,1)S(1)}, bf16[512,256]{1,0:T(8,128)(2,1)S(1)}, u32[]{:S(2)}, u32[]{:S(2)}) collective-permute-start(bf16[512,256]{1,0:T(8,128)(2,1)S(1)} %bitcast.18), channel_id=1, source_target_pairs={{0,1},{1,2},{2,3},{3,4},{4,5},{5,6},{6,7},{7,8},{8,9},{9,10},{10,1... | collective-permute-start | bytes 786440 | tf_op jit(solution)/shard_map/ppermute | solution.py:241
  11.3 2.7 %collective-permute-start.1 = (s32[1,16]{1,0:T(1,128)S(1)}, s32[1,16]{1,0:T(1,128)S(1)}, u32[]{:S(2)}, u32[]{:S(2)}) collective-permute-start(s32[1,16]{1,0:T(1,128)S(1)} %copy-done.4), channel_id=1, source_target_pairs={{0,64},{16,80},{32,96},{48,112},{64,0},{80,16},{96,32},{112,48},{1... | collective-permute-start | bytes 200 | tf_op jit(solution)/shard_map/ppermute | solution.py:269
  14.0 3.6 %collective-permute-start.2 = (s32[1,16]{1,0:T(1,128)S(1)}, s32[1,16]{1,0:T(1,128)S(1)}, u32[]{:S(2)}, u32[]{:S(2)}) collective-permute-start(s32[1,16]{1,0:T(1,128)S(1)} %add.15), channel_id=1, source_target_pairs={{0,192},{16,208},{32,224},{48,240},{64,128},{80,144},{96,160},{112... | collective-permute-start | bytes 200 | tf_op jit(solution)/shard_map/ppermute | solution.py:273
  17.6 27.5 %collective-permute-start.3 = (s32[1,16]{1,0:T(1,128)S(1)}, s32[1,16]{1,0:T(1,128)S(1)}, u32[]{:S(2)}, u32[]{:S(2)}) collective-permute-start(s32[1,16]{1,0:T(1,128)S(1)} %add.16), channel_id=1, source_target_pairs={{0,16},{16,0},{32,48},{48,32},{64,80},{80,64},{96,112},{112,96},{1... | collective-permute-start | bytes 200 | tf_op jit(solution)/shard_map/ppermute | solution.py:274
  20.6 0.7 %copy-start.3 = (bf16[512,256]{1,0:T(8,128)(2,1)}, bf16[512,256]{1,0:T(8,128)(2,1)S(1)}, u32[]{:S(2)}) copy-start(bf16[512,256]{1,0:T(8,128)(2,1)S(1)} %collective-permute-done.prev_ref) | copy-start | bytes 786436
  20.6 0.8 %copy-start.1 = (bf16[16,48,256]{2,1,0:T(8,128)(2,1)}, bf16[16,48,256]{2,1,0:T(8,128)(2,1)S(1)}, u32[]{:S(2)}) copy-start(bf16[16,48,256]{2,1,0:T(8,128)(2,1)S(1)} %all-to-all-done) | copy-start | bytes 1179652
  45.1 19.6 %all-to-all-start.1 = ((bf16[16,48,256]{2,1,0:T(8,128)(2,1)}), bf16[16,48,256]{2,1,0:T(8,128)(2,1)S(1)}, u32[]{:S(2)}, u32[]{:S(2)}) async-start(bf16[16,48,256]{2,1,0:T(8,128)(2,1)} %get-tuple-element.17), calls=%async_computation.1 | async-start | bytes 786432 | tf_op jit(solution)/shard_map/all_to_all | solution.py:245
  51.6 8.3 %collective-permute-start.4 = (s32[1,16]{1,0:T(1,128)S(1)}, s32[1,16]{1,0:T(1,128)S(1)}, u32[]{:S(2)}, u32[]{:S(2)}) collective-permute-start(s32[1,16]{1,0:T(1,128)S(1)} %add.17), channel_id=1, source_target_pairs={{0,48},{16,32},{32,16},{48,0},{64,112},{80,96},{96,80},{112,64},{1... | collective-permute-start | bytes 200 | tf_op jit(solution)/shard_map/ppermute | solution.py:282
  55.0 8.8 %collective-permute-start.5 = (bf16[512,256]{1,0:T(8,128)(2,1)}, bf16[512,256]{1,0:T(8,128)(2,1)S(1)}, u32[]{:S(2)}, u32[]{:S(2)}) collective-permute-start(bf16[512,256]{1,0:T(8,128)(2,1)} %get-tuple-element.16), channel_id=1, source_target_pairs={{0,15},{1,0},{2,1},{3,2},{4,3},{5,4},{6,5},{7,6},{8,7},{9,8},{10,9... | collective-permute-start | bytes 786440 | tf_op jit(solution)/shard_map/ppermute | solution.py:241
  61.3 2.5 %copy-start = (f32[512,256]{1,0:T(8,128)S(1)}, f32[512,256]{1,0:T(8,128)}, u32[]{:S(2)}) copy-start(f32[512,256]{1,0:T(8,128)} %get-tuple-element.15) | copy-start | bytes 1572868

commit v3 on v2

--- a/solution.py
+++ b/solution.py
@@ -205,7 +205,7 @@
         out_shape=[shape for _, shape in outs],
         scratch_shapes=[pltpu.VMEM(shape, dtype) for shape, dtype in scratch],
         compiler_params=pltpu.CompilerParams(
-            dimension_semantics=("arbitrary",), vmem_limit_bytes=56 * 2**20
+            dimension_semantics=("arbitrary",), vmem_limit_bytes=50 * 2**20
         ),
         cost_estimate=pl.CostEstimate(flops=flops, bytes_accessed=traffic, transcendentals=0),
     )

time: 65.7 us -> 62.9 us (0.957)
  other arithmetic: 4.64 us -> 3.36 us
  local copies, waits for them, and re-layouts: 2.4 us -> 1.56 us
  Pallas kernels: 23.7 us -> 23 us
    broadcast_in_dim x1, other arithmetic: 2.47 us -> 1.18 us  [body(): grad_query[None]]
    unnamed x10 -> x4, local copies, waits for them, and re-layouts: 0.86 us -> 0.01 us
  transfers between devices with their start and end apart: 8 -> 8, of which waited for: 3 -> 3; matrix products, arithmetic and copies ran while one was open for 6% -> 4% of each run, Pallas kernels for 36% -> 37%
where the time goes in v3:
time: 62.9 us; the launch traced here: 62.5 us
  starting transfers between devices  26.1 us (41%)
  Pallas kernels  23 us (37%)
  waiting for transfers between devices  7.07 us (11%)
  other arithmetic  3.36 us (5%)
  local copies, waits for them, and re-layouts  1.56 us (2%)
  between operations  1.36 us (2%)
    pallas_call x1, Pallas kernels, body(): core(lengths, shard, queries[0], upstream[0], prefix_all, prev, resp_kv[0])  23 us
    all_to_all x2, starting transfers between devices, exchange(): lax.all_to_all(packets, 'seq', split_axis=0, concat_axis=0, tiled=True)  13.9 us
    ppermute x1, waiting for transfers between devices, body(): counts = counts + lax.ppermute(counts, 'prompt', fourth)  4.46 us
    ppermute x1, starting transfers between devices, body(): counts = counts + lax.ppermute(counts, 'prompt', fourth)  3.39 us
    ppermute x1, starting transfers between devices, body(): incoming = lax.ppermute(counts, 'prompt', third)  2.99 us
    ppermute x1, starting transfers between devices, body(): counts = counts + lax.ppermute(counts, 'prompt', second)  2.48 us
    ppermute x2, starting transfers between devices, ring(): lax.ppermute(block, 'seq', [(i, (i + distance) % size) for i in range(siz...  2.2 us
    broadcast_in_dim x1, local copies, waits for them, and re-layouts, body(): prefix_all = exchange(jnp.broadcast_to(prefix_kv, (n_seq, part, 2 * DH)))  1.55 us
  transfers between devices with their start and end apart: 8, of which 3 were waited for; matrix products, arithmetic and copies ran while one was open for 4% of the time, Pallas kernels for 37%

profile of v3, /device:TPU:1, one launch (start us, length us, event | category | flops | bytes accessed | tf_op | source)
XLA Modules:
  0.0 62.5 jit_solution(5871646700780822912)
XLA Ops:
  0.6 0.0 copy-start
  0.6 0.0 copy-start.1
  0.7 1.5 %broadcast_in_dim.22 = bf16[16,48,256]{2,1,0:T(8,128)(2,1)} broadcast(bf16[48,256]{1,0:T(8,128)(2,1)} %bitcast.16), dimensions={1,2} | broadcast | bytes 417792 | tf_op jit(solution)/shard_map/broadcast_in_dim | solution.py:271
  2.2 7.3 %all-to-all-start = ((bf16[16,48,256]{2,1,0:T(8,128)(2,1)}), bf16[16,48,256]{2,1,0:T(8,128)(2,1)S(1)}, u32[]{:S(2)}, u32[]{:S(2)}) async-start(bf16[16,48,256]{2,1,0:T(8,128)(2,1)} %broadcast_in_dim.22), calls=%async_computation | async-start | bytes 786432 | tf_op jit(solution)/shard_map/all_to_all | solution.py:245
  9.5 0.0 copy-done
  9.5 1.7 %collective-permute-start = (bf16[512,256]{1,0:T(8,128)(2,1)S(1)}, bf16[512,256]{1,0:T(8,128)(2,1)S(1)}, u32[]{:S(2)}, u32[]{:S(2)}) collective-permute-start(bf16[512,256]{1,0:T(8,128)(2,1)S(1)} %bitcast.14), channel_id=1, source_target_pairs={{0,1},{1,2},{2,3},{3,4},{4,5},{5,6},{6,7},{7,8},{8,9},{9,10},{10,1... | collective-permute-start | bytes 786440 | tf_op jit(solution)/shard_map/ppermute | solution.py:241
  11.3 0.0 copy-done.1
  11.3 1.2 %collective-permute-start.1 = (s32[1,16]{1,0:T(1,128)S(1)}, s32[1,16]{1,0:T(1,128)S(1)}, u32[]{:S(2)}, u32[]{:S(2)}) collective-permute-start(s32[1,16]{1,0:T(1,128)S(1)} %copy-done.1), channel_id=1, source_target_pairs={{0,64},{16,80},{32,96},{48,112},{64,0},{80,16},{96,32},{112,48},{1... | collective-permute-start | bytes 200 | tf_op jit(solution)/shard_map/ppermute | solution.py:269
  12.5 1.5 %collective-permute-done.1 = s32[1,16]{1,0:T(1,128)S(1)} collective-permute-done((s32[1,16]{1,0:T(1,128)S(1)}, s32[1,16]{1,0:T(1,128)S(1)}, u32[]{:S(2)}, u32[]{:S(2)}) %collective-permute-start.1) | collective-permute-done | bytes 96 | tf_op jit(solution)/shard_map/ppermute | solution.py:269
  13.9 2.5 %collective-permute-start.2 = (s32[1,16]{1,0:T(1,128)S(1)}, s32[1,16]{1,0:T(1,128)S(1)}, u32[]{:S(2)}, u32[]{:S(2)}) collective-permute-start(s32[1,16]{1,0:T(1,128)S(1)} %add.15), channel_id=1, source_target_pairs={{0,192},{16,208},{32,224},{48,240},{64,128},{80,144},{96,160},{112... | collective-permute-start | bytes 200 | tf_op jit(solution)/shard_map/ppermute | solution.py:273
  16.4 1.1 %collective-permute-done.2 = s32[1,16]{1,0:T(1,128)S(1)} collective-permute-done((s32[1,16]{1,0:T(1,128)S(1)}, s32[1,16]{1,0:T(1,128)S(1)}, u32[]{:S(2)}, u32[]{:S(2)}) %collective-permute-start.2) | collective-permute-done | bytes 96 | tf_op jit(solution)/shard_map/ppermute | solution.py:273
  17.6 3.0 %collective-permute-start.3 = (s32[1,16]{1,0:T(1,128)S(1)}, s32[1,16]{1,0:T(1,128)S(1)}, u32[]{:S(2)}, u32[]{:S(2)}) collective-permute-start(s32[1,16]{1,0:T(1,128)S(1)} %add.16), channel_id=1, source_target_pairs={{0,16},{16,0},{32,48},{48,32},{64,80},{80,64},{96,112},{112,96},{1... | collective-permute-start | bytes 200 | tf_op jit(solution)/shard_map/ppermute | solution.py:274
  20.5 0.0 collective-permute-done.prev_ref
  20.5 0.0 all-to-all-done
  20.6 23.0 %attend.1 = (bf16[512,1024]{1,0:T(8,128)(2,1)}, bf16[512,1024]{1,0:T(8,128)(2,1)S(1)}, bf16[16,48,256]{2,1,0:T(8,128)(2,1)}, bf16[512,256]{1,0:T(8,128)(2,1)S(1)}, f32[512,256]{1,0:T(8,128)S(1)}) custom-call(s32[1,16]{1,0:T(1,128)S(1)} %copy-done.1, s32[1]{0:T(128)} %bitcast.shard_ref, bf16[512,1024]{1,0:T(8,128)(2,1)} %bitcast.17, ...), custom_call_target="tpu_custom_call" | custom-call | flops 8858370048 | bytes 6291456 | tf_op jit(solution)/shard_map/attend/pallas_call | solution.py:275
  43.6 0.0 collective-permute-done.3
  43.6 6.5 %all-to-all-start.1 = ((bf16[16,48,256]{2,1,0:T(8,128)(2,1)}), bf16[16,48,256]{2,1,0:T(8,128)(2,1)S(1)}, u32[]{:S(2)}, u32[]{:S(2)}) async-start(bf16[16,48,256]{2,1,0:T(8,128)(2,1)} %get-tuple-element.17), calls=%async_computation.1 | async-start | bytes 786432 | tf_op jit(solution)/shard_map/all_to_all | solution.py:245
  50.1 3.4 %collective-permute-start.4 = (s32[1,16]{1,0:T(1,128)S(1)}, s32[1,16]{1,0:T(1,128)S(1)}, u32[]{:S(2)}, u32[]{:S(2)}) collective-permute-start(s32[1,16]{1,0:T(1,128)S(1)} %add.17), channel_id=1, source_target_pairs={{0,48},{16,32},{32,16},{48,0},{64,112},{80,96},{96,80},{112,64},{1... | collective-permute-start | bytes 200 | tf_op jit(solution)/shard_map/ppermute | solution.py:282
  53.5 0.5 collective-permute-start.5
  54.0 4.5 %collective-permute-done.4 = s32[1,16]{1,0:T(1,128)S(1)} collective-permute-done((s32[1,16]{1,0:T(1,128)S(1)}, s32[1,16]{1,0:T(1,128)S(1)}, u32[]{:S(2)}, u32[]{:S(2)}) %collective-permute-start.4) | collective-permute-done | bytes 96 | tf_op jit(solution)/shard_map/ppermute | solution.py:282
  58.5 0.6 %add_reduce_fusion = s32[]{:T(128)} fusion(s32[1,16]{1,0:T(1,128)S(1)} %add.17, s32[1,16]{1,0:T(1,128)S(1)} %collective-permute-done.4), kind=kLoop, calls=%fused_computation.5 | loop fusion | flops 31 | bytes 132 | tf_op jit(solution)/shard_map/reduce_sum | solution.py:283
  59.8 1.2 %fusion = bf16[1,512,1024]{2,1,0:T(8,128)(2,1)} fusion(bf16[512,1024]{1,0:T(8,128)(2,1)S(1)} %get-tuple-element.12, f32[]{:T(128)S(6)} %div.3), kind=kLoop, calls=%fused_computation.1 | loop fusion | flops 1572864 | bytes 2097156 | tf_op jit(solution)/shard_map/broadcast_in_dim | solution.py:287
  61.0 0.0 collective-permute-done.5
  61.0 0.8 %multiply_bitcast_fusion = f32[1,512,256]{2,1,0:T(8,128)} fusion(f32[512,256]{1,0:T(8,128)S(1)} %get-tuple-element.15, bf16[512,256]{1,0:T(8,128)(2,1)S(1)} %collective-permute-done.5, f32[]{:T(128)S(6)} %div.3), kind=kLoop, calls=%fused_computation.3 | loop fusion | flops 393216 | bytes 1310724 | tf_op jit(solution)/shard_map/broadcast_in_dim | solution.py:287
  61.8 0.0 all-to-all-done.1
  61.8 0.1 convert_reduce_fusion
  61.9 0.6 %multiply_bitcast_fusion.1 = f32[1,48,256]{2,1,0:T(8,128)} fusion(f32[48,256]{1,0:T(8,128)S(1)} %convert_reduce_fusion, f32[]{:T(128)S(6)} %div.3), kind=kLoop, calls=%fused_computation.4 | loop fusion | flops 12288 | bytes 98308 | tf_op jit(solution)/shard_map/mul | solution.py:285
  (3 shorter events, 0.0 us)
Async XLA Ops:
  0.6 8.9 %copy-start = (bf16[1,512,256]{2,1,0:T(8,128)(2,1)S(1)}, bf16[1,512,256]{2,1,0:T(8,128)(2,1)}, u32[]{:S(2)}) copy-start(bf16[1,512,256]{2,1,0:T(8,128)(2,1)} %param.6) | copy-start | bytes 786436
  0.6 10.6 %copy-start.1 = (s32[1,16]{1,0:T(1,128)S(1)}, s32[1,16]{1,0:T(1,128)}, u32[]{:S(2)}) copy-start(s32[1,16]{1,0:T(1,128)} %len_ref.1) | copy-start | bytes 196
  2.2 18.4 %all-to-all-start = ((bf16[16,48,256]{2,1,0:T(8,128)(2,1)}), bf16[16,48,256]{2,1,0:T(8,128)(2,1)S(1)}, u32[]{:S(2)}, u32[]{:S(2)}) async-start(bf16[16,48,256]{2,1,0:T(8,128)(2,1)} %broadcast_in_dim.22), calls=%async_computation | async-start | bytes 786432 | tf_op jit(solution)/shard_map/all_to_all | solution.py:245
  9.5 11.0 %collective-permute-start = (bf16[512,256]{1,0:T(8,128)(2,1)S(1)}, bf16[512,256]{1,0:T(8,128)(2,1)S(1)}, u32[]{:S(2)}, u32[]{:S(2)}) collective-permute-start(bf16[512,256]{1,0:T(8,128)(2,1)S(1)} %bitcast.14), channel_id=1, source_target_pairs={{0,1},{1,2},{2,3},{3,4},{4,5},{5,6},{6,7},{7,8},{8,9},{9,10},{10,1... | collective-permute-start | bytes 786440 | tf_op jit(solution)/shard_map/ppermute | solution.py:241
  11.3 2.7 %collective-permute-start.1 = (s32[1,16]{1,0:T(1,128)S(1)}, s32[1,16]{1,0:T(1,128)S(1)}, u32[]{:S(2)}, u32[]{:S(2)}) collective-permute-start(s32[1,16]{1,0:T(1,128)S(1)} %copy-done.1), channel_id=1, source_target_pairs={{0,64},{16,80},{32,96},{48,112},{64,0},{80,16},{96,32},{112,48},{1... | collective-permute-start | bytes 200 | tf_op jit(solution)/shard_map/ppermute | solution.py:269
  13.9 3.6 %collective-permute-start.2 = (s32[1,16]{1,0:T(1,128)S(1)}, s32[1,16]{1,0:T(1,128)S(1)}, u32[]{:S(2)}, u32[]{:S(2)}) collective-permute-start(s32[1,16]{1,0:T(1,128)S(1)} %add.15), channel_id=1, source_target_pairs={{0,192},{16,208},{32,224},{48,240},{64,128},{80,144},{96,160},{112... | collective-permute-start | bytes 200 | tf_op jit(solution)/shard_map/ppermute | solution.py:273
  17.6 26.0 %collective-permute-start.3 = (s32[1,16]{1,0:T(1,128)S(1)}, s32[1,16]{1,0:T(1,128)S(1)}, u32[]{:S(2)}, u32[]{:S(2)}) collective-permute-start(s32[1,16]{1,0:T(1,128)S(1)} %add.16), channel_id=1, source_target_pairs={{0,16},{16,0},{32,48},{48,32},{64,80},{80,64},{96,112},{112,96},{1... | collective-permute-start | bytes 200 | tf_op jit(solution)/shard_map/ppermute | solution.py:274
  43.6 18.2 %all-to-all-start.1 = ((bf16[16,48,256]{2,1,0:T(8,128)(2,1)}), bf16[16,48,256]{2,1,0:T(8,128)(2,1)S(1)}, u32[]{:S(2)}, u32[]{:S(2)}) async-start(bf16[16,48,256]{2,1,0:T(8,128)(2,1)} %get-tuple-element.17), calls=%async_computation.1 | async-start | bytes 786432 | tf_op jit(solution)/shard_map/all_to_all | solution.py:245
  50.1 8.3 %collective-permute-start.4 = (s32[1,16]{1,0:T(1,128)S(1)}, s32[1,16]{1,0:T(1,128)S(1)}, u32[]{:S(2)}, u32[]{:S(2)}) collective-permute-start(s32[1,16]{1,0:T(1,128)S(1)} %add.17), channel_id=1, source_target_pairs={{0,48},{16,32},{32,16},{48,0},{64,112},{80,96},{96,80},{112,64},{1... | collective-permute-start | bytes 200 | tf_op jit(solution)/shard_map/ppermute | solution.py:282
  53.5 7.5 %collective-permute-start.5 = (bf16[512,256]{1,0:T(8,128)(2,1)S(1)}, bf16[512,256]{1,0:T(8,128)(2,1)S(1)}, u32[]{:S(2)}, u32[]{:S(2)}) collective-permute-start(bf16[512,256]{1,0:T(8,128)(2,1)S(1)} %get-tuple-element.16), channel_id=1, source_target_pairs={{0,15},{1,0},{2,1},{3,2},{4,3},{5,4},{6,5},{7,6},{8,7},{9,8},{10,9... | collective-permute-start | bytes 786440 | tf_op jit(solution)/shard_map/ppermute | solution.py:241

commit v4 on v3

--- a/solution.py
+++ b/solution.py
@@ -251,8 +251,7 @@
     def paired(k, odd):
         return ((k + odd) ^ 1) - odd
 
-    for odd in (0, 1):
-        yield [(p, (paired(p // side, odd) % side) * side + p % side) for p in range(n_prompt)]
+    yield [[(p, (p + turn * side) % n_prompt) for p in range(n_prompt)] for turn in range(1, side)]
     for odd in (0, 1):
         yield [(p, p // side * side + paired(p % side, odd) % side) for p in range(n_prompt)]
 
@@ -264,13 +263,12 @@
     shard = lax.axis_index("seq").astype(jnp.int32)[None]
     part = prefix_kv.shape[1]
     core = kernels(rows, n_seq * part, width // DH, n_seq)
-    first, second, third, fourth = pair_routes(n_prompt)
+    across, third, fourth = pair_routes(n_prompt)
     counts = lengths
-    counts = counts + lax.ppermute(counts, "prompt", first)
+    counts = counts + sum(lax.ppermute(lengths, "prompt", route) for route in across)
     prev = ring(resp_kv[0], 1)
     prefix_all = exchange(jnp.broadcast_to(prefix_kv, (n_seq, part, 2 * DH)))
     prefix_all = prefix_all.reshape(n_seq * part, 2 * DH)
-    counts = counts + lax.ppermute(counts, "prompt", second)
     incoming = lax.ppermute(counts, "prompt", third)
     attended, grad_query, packet, g_prev, g_own = core(
         lengths, shard, queries[0], upstream[0], prefix_all, prev, resp_kv[0]

time: 62.9 us -> 63.1 us (level)
  starting transfers between devices: 26.1 us -> 27.5 us
  waiting for transfers between devices: 7.07 us -> 5.99 us
    ppermute x2 -> x3, waiting for transfers between devices: 2.6 us -> 1.24 us  [body(): lax.ppermute(lengths, 'prompt', route)]
    ppermute x2 -> x3, starting transfers between devices: 3.69 us -> 4.81 us  [body(): lax.ppermute(lengths, 'prompt', route)]
  transfers between devices with their start and end apart: 8 -> 9, of which waited for: 3 -> 3; matrix products, arithmetic and copies ran while one was open for 4% -> 4% of each run, Pallas kernels for 37% -> 37%
where the time goes in v4:
time: 63.1 us; the launch traced here: 62.8 us
  starting transfers between devices  27.5 us (44%)
  Pallas kernels  23 us (36%)
  waiting for transfers between devices  5.99 us (9%)
  other arithmetic  3.36 us (5%)
  local copies, waits for them, and re-layouts  1.56 us (2%)
  between operations  1.36 us (2%)
    pallas_call x1, Pallas kernels, body(): core(lengths, shard, queries[0], upstream[0], prefix_all, prev, resp_kv[0])  23 us
    all_to_all x2, starting transfers between devices, exchange(): lax.all_to_all(packets, 'seq', split_axis=0, concat_axis=0, tiled=True)  13.6 us
    ppermute x3, starting transfers between devices, body(): lax.ppermute(lengths, 'prompt', route)  4.81 us
    ppermute x1, waiting for transfers between devices, body(): counts = counts + lax.ppermute(counts, 'prompt', fourth)  4.74 us
    ppermute x1, starting transfers between devices, body(): counts = counts + lax.ppermute(counts, 'prompt', fourth)  3.91 us
    ppermute x1, starting transfers between devices, body(): incoming = lax.ppermute(counts, 'prompt', third)  2.99 us
    ppermute x2, starting transfers between devices, ring(): lax.ppermute(block, 'seq', [(i, (i + distance) % size) for i in range(siz...  2.21 us
    broadcast_in_dim x1, local copies, waits for them, and re-layouts, body(): prefix_all = exchange(jnp.broadcast_to(prefix_kv, (n_seq, part, 2 * DH)))  1.55 us
  transfers between devices with their start and end apart: 9, of which 3 were waited for; matrix products, arithmetic and copies ran while one was open for 4% of the time, Pallas kernels for 37%

profile of v4, /device:TPU:1, one launch (start us, length us, event | category | flops | bytes accessed | tf_op | source)
XLA Modules:
  0.0 62.8 jit_solution(3812205166045849642)
XLA Ops:
  0.6 0.0 copy-start.1
  0.6 0.0 copy-start
  0.7 1.5 %broadcast_in_dim.22 = bf16[16,48,256]{2,1,0:T(8,128)(2,1)} broadcast(bf16[48,256]{1,0:T(8,128)(2,1)} %bitcast.16), dimensions={1,2} | broadcast | bytes 417792 | tf_op jit(solution)/shard_map/broadcast_in_dim | solution.py:270
  2.2 7.3 %all-to-all-start = ((bf16[16,48,256]{2,1,0:T(8,128)(2,1)}), bf16[16,48,256]{2,1,0:T(8,128)(2,1)S(1)}, u32[]{:S(2)}, u32[]{:S(2)}) async-start(bf16[16,48,256]{2,1,0:T(8,128)(2,1)} %broadcast_in_dim.22), calls=%async_computation | async-start | bytes 786432 | tf_op jit(solution)/shard_map/all_to_all | solution.py:245
  9.5 0.0 copy-done.1
  9.5 1.7 %collective-permute-start = (bf16[512,256]{1,0:T(8,128)(2,1)S(1)}, bf16[512,256]{1,0:T(8,128)(2,1)S(1)}, u32[]{:S(2)}, u32[]{:S(2)}) collective-permute-start(bf16[512,256]{1,0:T(8,128)(2,1)S(1)} %bitcast.14), channel_id=1, source_target_pairs={{0,1},{1,2},{2,3},{3,4},{4,5},{5,6},{6,7},{7,8},{8,9},{9,10},{10,1... | collective-permute-start | bytes 786440 | tf_op jit(solution)/shard_map/ppermute | solution.py:241
  11.3 0.0 copy-done
  11.3 1.2 %collective-permute-start.1 = (s32[1,16]{1,0:T(1,128)S(1)}, s32[1,16]{1,0:T(1,128)S(1)}, u32[]{:S(2)}, u32[]{:S(2)}) collective-permute-start(s32[1,16]{1,0:T(1,128)S(1)} %copy-done), channel_id=1, source_target_pairs={{0,64},{16,80},{32,96},{48,112},{64,128},{80,144},{96,160},{112,17... | collective-permute-start | bytes 200 | tf_op jit(solution)/shard_map/ppermute | solution.py:268
  12.5 2.5 %collective-permute-start.2 = (s32[1,16]{1,0:T(1,128)S(1)}, s32[1,16]{1,0:T(1,128)S(1)}, u32[]{:S(2)}, u32[]{:S(2)}) collective-permute-start(s32[1,16]{1,0:T(1,128)S(1)} %copy-done), channel_id=1, source_target_pairs={{0,128},{16,144},{32,160},{48,176},{64,192},{80,208},{96,224},{112... | collective-permute-start | bytes 200 | tf_op jit(solution)/shard_map/ppermute | solution.py:268
  14.9 1.2 %collective-permute-start.3 = (s32[1,16]{1,0:T(1,128)S(1)}, s32[1,16]{1,0:T(1,128)S(1)}, u32[]{:S(2)}, u32[]{:S(2)}) collective-permute-start(s32[1,16]{1,0:T(1,128)S(1)} %copy-done), channel_id=1, source_target_pairs={{0,192},{16,208},{32,224},{48,240},{64,0},{80,16},{96,32},{112,48}... | collective-permute-start | bytes 200 | tf_op jit(solution)/shard_map/ppermute | solution.py:268
  16.1 0.0 collective-permute-done.1
  16.1 0.6 collective-permute-done.2
  16.7 0.7 %collective-permute-done.3 = s32[1,16]{1,0:T(1,128)S(1)} collective-permute-done((s32[1,16]{1,0:T(1,128)S(1)}, s32[1,16]{1,0:T(1,128)S(1)}, u32[]{:S(2)}, u32[]{:S(2)}) %collective-permute-start.3) | collective-permute-done | bytes 96 | tf_op jit(solution)/shard_map/ppermute | solution.py:268
  17.3 3.0 %collective-permute-start.4 = (s32[1,16]{1,0:T(1,128)S(1)}, s32[1,16]{1,0:T(1,128)S(1)}, u32[]{:S(2)}, u32[]{:S(2)}) collective-permute-start(s32[1,16]{1,0:T(1,128)S(1)} %add_add_fusion), channel_id=1, source_target_pairs={{0,16},{16,0},{32,48},{48,32},{64,80},{80,64},{96,112},{112,96},{1... | collective-permute-start | bytes 200 | tf_op jit(solution)/shard_map/ppermute | solution.py:272
  20.3 0.0 collective-permute-done.prev_ref
  20.3 0.0 all-to-all-done
  20.3 23.0 %attend.1 = (bf16[512,1024]{1,0:T(8,128)(2,1)}, bf16[512,1024]{1,0:T(8,128)(2,1)S(1)}, bf16[16,48,256]{2,1,0:T(8,128)(2,1)}, bf16[512,256]{1,0:T(8,128)(2,1)S(1)}, f32[512,256]{1,0:T(8,128)S(1)}) custom-call(s32[1,16]{1,0:T(1,128)S(1)} %copy-done, s32[1]{0:T(128)} %bitcast.shard_ref, bf16[512,1024]{1,0:T(8,128)(2,1)} %bitcast.17, ...), custom_call_target="tpu_custom_call" | custom-call | flops 8858370048 | bytes 6291456 | tf_op jit(solution)/shard_map/attend/pallas_call | solution.py:273
  43.3 0.0 collective-permute-done.4
  43.3 6.2 %all-to-all-start.1 = ((bf16[16,48,256]{2,1,0:T(8,128)(2,1)}), bf16[16,48,256]{2,1,0:T(8,128)(2,1)S(1)}, u32[]{:S(2)}, u32[]{:S(2)}) async-start(bf16[16,48,256]{2,1,0:T(8,128)(2,1)} %get-tuple-element.17), calls=%async_computation.1 | async-start | bytes 786432 | tf_op jit(solution)/shard_map/all_to_all | solution.py:245
  49.6 3.9 %collective-permute-start.5 = (s32[1,16]{1,0:T(1,128)S(1)}, s32[1,16]{1,0:T(1,128)S(1)}, u32[]{:S(2)}, u32[]{:S(2)}) collective-permute-start(s32[1,16]{1,0:T(1,128)S(1)} %add.21), channel_id=1, source_target_pairs={{0,48},{16,32},{32,16},{48,0},{64,112},{80,96},{96,80},{112,64},{1... | collective-permute-start | bytes 200 | tf_op jit(solution)/shard_map/ppermute | solution.py:280
  53.5 0.5 collective-permute-start.6
  54.0 4.7 %collective-permute-done.5 = s32[1,16]{1,0:T(1,128)S(1)} collective-permute-done((s32[1,16]{1,0:T(1,128)S(1)}, s32[1,16]{1,0:T(1,128)S(1)}, u32[]{:S(2)}, u32[]{:S(2)}) %collective-permute-start.5) | collective-permute-done | bytes 96 | tf_op jit(solution)/shard_map/ppermute | solution.py:280
  58.7 0.6 %add_reduce_fusion = s32[]{:T(128)} fusion(s32[1,16]{1,0:T(1,128)S(1)} %add.21, s32[1,16]{1,0:T(1,128)S(1)} %collective-permute-done.5), kind=kLoop, calls=%fused_computation.5 | loop fusion | flops 31 | bytes 132 | tf_op jit(solution)/shard_map/reduce_sum | solution.py:281
  60.1 1.2 %fusion = bf16[1,512,1024]{2,1,0:T(8,128)(2,1)} fusion(bf16[512,1024]{1,0:T(8,128)(2,1)S(1)} %get-tuple-element.12, f32[]{:T(128)S(6)} %div.3), kind=kLoop, calls=%fused_computation.1 | loop fusion | flops 1572864 | bytes 2097156 | tf_op jit(solution)/shard_map/broadcast_in_dim | solution.py:285
  61.3 0.0 collective-permute-done.6
  61.3 0.8 %multiply_bitcast_fusion = f32[1,512,256]{2,1,0:T(8,128)} fusion(f32[512,256]{1,0:T(8,128)S(1)} %get-tuple-element.15, bf16[512,256]{1,0:T(8,128)(2,1)S(1)} %collective-permute-done.6, f32[]{:T(128)S(6)} %div.3), kind=kLoop, calls=%fused_computation.3 | loop fusion | flops 393216 | bytes 1310724 | tf_op jit(solution)/shard_map/broadcast_in_dim | solution.py:285
  62.1 0.0 all-to-all-done.1
  62.1 0.1 convert_reduce_fusion
  62.2 0.6 multiply_bitcast_fusion.1
  (2 shorter events, 0.0 us)
Async XLA Ops:
  0.6 8.9 %copy-start.1 = (bf16[1,512,256]{2,1,0:T(8,128)(2,1)S(1)}, bf16[1,512,256]{2,1,0:T(8,128)(2,1)}, u32[]{:S(2)}) copy-start(bf16[1,512,256]{2,1,0:T(8,128)(2,1)} %param.6) | copy-start | bytes 786436
  0.6 10.6 %copy-start = (s32[1,16]{1,0:T(1,128)S(1)}, s32[1,16]{1,0:T(1,128)}, u32[]{:S(2)}) copy-start(s32[1,16]{1,0:T(1,128)} %len_ref.1) | copy-start | bytes 196
  2.2 18.1 %all-to-all-start = ((bf16[16,48,256]{2,1,0:T(8,128)(2,1)}), bf16[16,48,256]{2,1,0:T(8,128)(2,1)S(1)}, u32[]{:S(2)}, u32[]{:S(2)}) async-start(bf16[16,48,256]{2,1,0:T(8,128)(2,1)} %broadcast_in_dim.22), calls=%async_computation | async-start | bytes 786432 | tf_op jit(solution)/shard_map/all_to_all | solution.py:245
  9.5 10.8 %collective-permute-start = (bf16[512,256]{1,0:T(8,128)(2,1)S(1)}, bf16[512,256]{1,0:T(8,128)(2,1)S(1)}, u32[]{:S(2)}, u32[]{:S(2)}) collective-permute-start(bf16[512,256]{1,0:T(8,128)(2,1)S(1)} %bitcast.14), channel_id=1, source_target_pairs={{0,1},{1,2},{2,3},{3,4},{4,5},{5,6},{6,7},{7,8},{8,9},{9,10},{10,1... | collective-permute-start | bytes 786440 | tf_op jit(solution)/shard_map/ppermute | solution.py:241
  11.3 4.8 %collective-permute-start.1 = (s32[1,16]{1,0:T(1,128)S(1)}, s32[1,16]{1,0:T(1,128)S(1)}, u32[]{:S(2)}, u32[]{:S(2)}) collective-permute-start(s32[1,16]{1,0:T(1,128)S(1)} %copy-done), channel_id=1, source_target_pairs={{0,64},{16,80},{32,96},{48,112},{64,128},{80,144},{96,160},{112,17... | collective-permute-start | bytes 200 | tf_op jit(solution)/shard_map/ppermute | solution.py:268
  12.5 4.2 %collective-permute-start.2 = (s32[1,16]{1,0:T(1,128)S(1)}, s32[1,16]{1,0:T(1,128)S(1)}, u32[]{:S(2)}, u32[]{:S(2)}) collective-permute-start(s32[1,16]{1,0:T(1,128)S(1)} %copy-done), channel_id=1, source_target_pairs={{0,128},{16,144},{32,160},{48,176},{64,192},{80,208},{96,224},{112... | collective-permute-start | bytes 200 | tf_op jit(solution)/shard_map/ppermute | solution.py:268
  14.9 2.4 %collective-permute-start.3 = (s32[1,16]{1,0:T(1,128)S(1)}, s32[1,16]{1,0:T(1,128)S(1)}, u32[]{:S(2)}, u32[]{:S(2)}) collective-permute-start(s32[1,16]{1,0:T(1,128)S(1)} %copy-done), channel_id=1, source_target_pairs={{0,192},{16,208},{32,224},{48,240},{64,0},{80,16},{96,32},{112,48}... | collective-permute-start | bytes 200 | tf_op jit(solution)/shard_map/ppermute | solution.py:268
  17.3 26.0 %collective-permute-start.4 = (s32[1,16]{1,0:T(1,128)S(1)}, s32[1,16]{1,0:T(1,128)S(1)}, u32[]{:S(2)}, u32[]{:S(2)}) collective-permute-start(s32[1,16]{1,0:T(1,128)S(1)} %add_add_fusion), channel_id=1, source_target_pairs={{0,16},{16,0},{32,48},{48,32},{64,80},{80,64},{96,112},{112,96},{1... | collective-permute-start | bytes 200 | tf_op jit(solution)/shard_map/ppermute | solution.py:272
  43.3 18.8 %all-to-all-start.1 = ((bf16[16,48,256]{2,1,0:T(8,128)(2,1)}), bf16[16,48,256]{2,1,0:T(8,128)(2,1)S(1)}, u32[]{:S(2)}, u32[]{:S(2)}) async-start(bf16[16,48,256]{2,1,0:T(8,128)(2,1)} %get-tuple-element.17), calls=%async_computation.1 | async-start | bytes 786432 | tf_op jit(solution)/shard_map/all_to_all | solution.py:245
  49.6 9.2 %collective-permute-start.5 = (s32[1,16]{1,0:T(1,128)S(1)}, s32[1,16]{1,0:T(1,128)S(1)}, u32[]{:S(2)}, u32[]{:S(2)}) collective-permute-start(s32[1,16]{1,0:T(1,128)S(1)} %add.21), channel_id=1, source_target_pairs={{0,48},{16,32},{32,16},{48,0},{64,112},{80,96},{96,80},{112,64},{1... | collective-permute-start | bytes 200 | tf_op jit(solution)/shard_map/ppermute | solution.py:280
  53.5 7.8 %collective-permute-start.6 = (bf16[512,256]{1,0:T(8,128)(2,1)S(1)}, bf16[512,256]{1,0:T(8,128)(2,1)S(1)}, u32[]{:S(2)}, u32[]{:S(2)}) collective-permute-start(bf16[512,256]{1,0:T(8,128)(2,1)S(1)} %get-tuple-element.16), channel_id=1, source_target_pairs={{0,15},{1,0},{2,1},{3,2},{4,3},{5,4},{6,5},{7,6},{8,7},{9,8},{10,9... | collective-permute-start | bytes 786440 | tf_op jit(solution)/shard_map/ppermute | solution.py:241
